TPU v7x, 256 devices: a whole 4x4x8 slice. The times are simulated.
256 devices in a mesh: blk: 256 (over z, x, y, core).
Axes of the slice: x: 4, y: 4, z: 8, core: 2. Of those that a mesh axis runs over, the one named last changes fastest.
Arguments:
- points: float32 [11, 65536], P(None, 'blk'), may hold values from -6 to 6
- lengthscales: float32 [11], replicated, may hold values from 1.5 to 6
- noise: float32 [1], replicated, may hold values from 0.5 to 2
- solution: float32 [16, 65536], P(None, 'blk'), may hold values from -6 to 6
- residual: float32 [16, 65536], P(None, 'blk'), may hold values from -6 to 6
- direction: float32 [16, 65536], P(None, 'blk'), may hold values from -6 to 6
Outputs:
- solution_next: float32 [16, 65536], P(None, 'blk')
- residual_next: float32 [16, 65536], P(None, 'blk')
- direction_next: float32 [16, 65536], P(None, 'blk')
All inputs are finite; a program needn't handle non-finite values.
Results may differ from a plain program's by a relative error of at most 0.0003.
Values sent between devices are 32-bit elements; how exact they have to be, the bound alone decides.
A program may use at most 192 MiB of HBM per device.

v0:
```python
import jax
import jax.numpy as jnp
from jax import lax
from jax.sharding import PartitionSpec as P


def matern(left, right, lengthscales):
    scaled_left = left / lengthscales[:, None]
    scaled_right = right / lengthscales[:, None]
    dist_sq = jnp.zeros((left.shape[1], right.shape[1]), jnp.float32)
    for feature in range(left.shape[0]):
        diff = scaled_left[feature][:, None] - scaled_right[feature][None, :]
        dist_sq = dist_sq + diff * diff
    scaled = jnp.sqrt(5.0 * dist_sq)
    return (1.0 + scaled + scaled * scaled / 3.0) * jnp.exp(-scaled)


def apply_rows(vectors, tile):
    return lax.dot_general(
        vectors,
        tile,
        (((1,), (1,)), ((), ())),
        precision=lax.Precision.HIGHEST,
        preferred_element_type=jnp.float32,
    )


def on_device(points, lengthscales, noise, solution, residual, direction):
    tile = matern(points, lax.all_gather(points, "blk", axis=1, tiled=True), lengthscales)
    kernel_part = apply_rows(lax.all_gather(direction, "blk", axis=1, tiled=True), tile)
    image = kernel_part + noise[0] * direction
    norm_now = lax.psum(jnp.sum(residual * residual, axis=1), "blk")
    curv = lax.psum(jnp.sum(direction * image, axis=1), "blk")
    alpha = norm_now / curv
    solution_next = solution + alpha[:, None] * direction
    residual_next = residual - alpha[:, None] * image
    norm_next = lax.psum(jnp.sum(residual_next * residual_next, axis=1), "blk")
    direction_next = residual_next + (norm_next / norm_now)[:, None] * direction
    return (solution_next, residual_next, direction_next)


def solution(mesh):
    placed = (P(None, "blk"), P(), P(), P(None, "blk"), P(None, "blk"), P(None, "blk"))
    return jax.shard_map(
        on_device,
        mesh=mesh,
        in_specs=placed,
        out_specs=(P(None, "blk"), P(None, "blk"), P(None, "blk")),
        check_vma=False,
    )
```

profile of v0, /device:TPU:1, one launch (start us, length us, event | category | flops | bytes accessed | tf_op | source)
XLA Modules:
  0.0 460.8 jit_solution(14884651212819070093)
XLA Ops:
  7.2 0.0 copy-start
  7.2 0.0 all-gather.3.cloned.1.call-start
  7.2 0.7 all-gather.3.cloned.1.call-update
  7.9 0.0 all-gather.5.cloned.1.call-start
  8.0 0.7 all-gather.5.cloned.1.call-update
  8.7 0.8 broadcast_divide_fusion.1
  10.1 0.8 multiply_reduce_fusion.2
  11.0 112.4 %all-gather.3.cloned.1.call-done = f32[11,65536]{1,0:T(8,128)} async-done(((f32[11,256]{1,0:T(8,128)}), f32[11,65536]{1,0:T(8,128)}) %all-gather.3.cloned.1.call-update) | async-done | bytes 2883600 | tf_op jit(solution)/shard_map/all_gather | solution.py:29
  123.3 2.5 broadcast_divide_fusion
  125.9 2.2 fusion.76
  128.0 0.0 copy-start.1
  128.0 0.0 copy-start.3
  128.0 119.2 %fusion.72.clone.4 = f32[256,65536]{1,0:T(8,128)} fusion(f32[65536]{0:T(1024)S(1)} %bitcast.32, f32[256]{0:T(256)S(1)} %bitcast.43, f32[65536]{0:T(1024)S(1)} %bitcast.33, f32[256]{0:T(256)S(1)} %bitcast.44, f32[65536]{0:T(1024)S(1)} %bitcast.34, f32[256]{0:T(256)S(1)} %bitcast.45, f32[65536]{0:T(1024)S(1)} %bitcast.35, ...), kind=kLoop, calls=%fused_computation.1.clone.clone.clone.clone.clone.clone.clone.1 | loop fusion | flops 654311424 | bytes 70003712 | tf_op jit(solution)/shard_map/reduce_sum | solution.py:33
  247.2 0.0 all-gather.5.cloned.1.call-done
  247.2 0.0 copy-done
  247.2 56.5 %multiply_reduce_fusion.1 = (f32[16]{0:T(128)S(1)}, f32[16,256]{1,0:T(8,128)S(1)}) fusion(f32[16,256]{1,0:T(8,128)S(1)} %copy-done, f32[]{:T(128)} %bitcast.30, f32[16,65536]{1,0:T(8,128)} %all-gather.5.cloned.1.call-done, f32[256,65536]{1,0:T(8,128)} %fusion.72.clone.4), kind=kOutput, calls=%fused_computation.74 | convolution fusion | flops 3221241856 | bytes 71336000 | tf_op jit(solution)/shard_map/dot_general | solution.py:19
  303.7 77.1 %all-reduce = (f32[16]{0:T(128)S(1)}, f32[16]{0:T(128)S(1)}) all-reduce(f32[16]{0:T(128)S(1)} %multiply_reduce_fusion.2, f32[16]{0:T(128)S(1)} %get-tuple-element.31), channel_id=1, replica_groups=mesh['blk'=256] {'blk'}, use_global_device_ids=true, to_apply=%region_1.0 | all-reduce | flops 32 | bytes 256 | tf_op jit(solution)/shard_map/psum | solution.py:32
  380.8 0.0 copy-done.1
  380.8 0.2 multiply_reduce_fusion
  381.0 0.0 copy-start.2
  381.0 72.3 %psum.23 = f32[16]{0:T(128)S(1)} all-reduce(f32[16]{0:T(128)S(1)} %get-tuple-element.5), channel_id=1, replica_groups=mesh['blk'=256] {'blk'}, use_global_device_ids=true, to_apply=%region_5.0 | all-reduce | flops 16 | bytes 128 | tf_op jit(solution)/shard_map/psum | solution.py:37
  453.3 0.0 copy-done.3
  453.3 0.7 multiply_add_fusion
  454.0 0.0 copy-done.2
  (3 shorter events, 0.0 us)
Async XLA Ops:
  7.2 240.0 %copy-start = (f32[16,256]{1,0:T(8,128)S(1)}, f32[16,256]{1,0:T(8,128)}, u32[]{:S(2)}) copy-start(f32[16,256]{1,0:T(8,128)} %param.11) | copy-start | bytes 49156
  7.2 116.1 %all-gather.3.cloned.1.call-start = ((), (), s32[]{:S(2)}) async-start(), calls=%async_computation | async-start | bytes 4210688 | tf_op jit(solution)/shard_map/all_gather | solution.py:29
  7.9 239.3 %all-gather.5.cloned.1.call-start = ((), (), s32[]{:S(2)}) async-start(), calls=%async_computation.1 | async-start | bytes 4210688 | tf_op jit(solution)/shard_map/all_gather | solution.py:30
  128.0 252.8 %copy-start.1 = (f32[16,256]{1,0:T(8,128)S(1)}, f32[16,256]{1,0:T(8,128)}, u32[]{:S(2)}) copy-start(f32[16,256]{1,0:T(8,128)} %param.10) | copy-start | bytes 49156
  128.0 325.3 %copy-start.3 = (f32[16,256]{1,0:T(8,128)S(1)}, f32[16,256]{1,0:T(8,128)}, u32[]{:S(2)}) copy-start(f32[16,256]{1,0:T(8,128)} %param.9) | copy-start | bytes 49156
  381.0 73.0 %copy-start.2 = (f32[16,256]{1,0:T(8,128)}, f32[16,256]{1,0:T(8,128)S(1)}, u32[]{:S(2)}) copy-start(f32[16,256]{1,0:T(8,128)S(1)} %get-tuple-element.6) | copy-start | bytes 49156
Sparse Core Ops, SparseCore 0:
  11.8 111.4 all-gather.2
  127.1 106.4 all-gather.4
where the time goes:
time: 461 us
  blocking collectives  149 us (32%)
  other arithmetic  124 us (27%)
  waiting for transfers between devices  114 us (25%)
  matrix products  56.5 us (12%)
  between operations  14.7 us (3%)
    reduce_sum x1, other arithmetic, on_device(): curv = lax.psum(jnp.sum(direction * image, axis=1), 'blk')  119 us
    all_gather x1, waiting for transfers between devices, on_device(): lax.all_gather(points, 'blk', axis=1, tiled=True)  112 us
    psum x1, blocking collectives, on_device(): norm_now = lax.psum(jnp.sum(residual * residual, axis=1), 'blk')  77.1 us
    psum x1, blocking collectives, on_device(): norm_next = lax.psum(jnp.sum(residual_next * residual_next, axis=1), 'blk')  72.3 us
    dot_general x1, matrix products, apply_rows(): lax.dot_general(vectors, tile, (((1,), (1,)), ((), ())), precision=lax.Pr...  56.5 us
  transfers between devices with their start and end apart: 2, of which 1 were waited for; matrix products, arithmetic and copies ran while one was open for 27% of the time, Pallas kernels for 0%

commit v1 on v0

v1 whole, which is shorter than its diff:
```python
import math

import jax
import jax.numpy as jnp
from jax import lax
from jax.experimental import pallas as pl
from jax.experimental.pallas import tpu as pltpu
from jax.sharding import PartitionSpec as P

MESH = pl.DeviceIdType.MESH
F32, BF16 = jnp.float32, jnp.bfloat16
SIDE = 16
SLOTS = 9
LN2 = math.log(2.0)
SCALE = math.sqrt(5.0) / LN2
CURVE = LN2 * LN2 / 3.0
BEND = 3.0 / LN2
LIFT = 3.0 / (LN2 * LN2)
LAST = (((1,), (1,)), ((), ()))


def three(value):
    high = value.astype(BF16).astype(F32)
    rest = value - high
    middle = rest.astype(BF16).astype(F32)
    return high, middle, (rest - middle).astype(BF16).astype(F32)


def two(value):
    high = value.astype(BF16)
    return high, (value - high.astype(F32)).astype(BF16)


def matern(square):
    square = jnp.maximum(square, 1e-30)
    root = square * lax.rsqrt(square)
    return (square + BEND * root + LIFT) * jnp.exp2(-root)


def kernel(
    scales_ref, noise_ref, points_ref, sol_ref, res_ref, dir_ref,
    sol_out, res_out, dir_out,
    rows, cols, left, right, dir_row, dir_col, acc_row, acc_col, square, high, low,
    out_row, out_col, in_row, in_col, stat_col, stat_row,
    row_send, row_recv, col_send, col_recv, rs_row_send, rs_row_recv, rs_col_send, rs_col_recv,
    sc_send, sc_recv, sr_send, sr_recv,
):
    me = lax.axis_index("blk")
    down = lax.rem(me // 2, SIDE)
    across = (me // (2 * SIDE)) * 2 + lax.rem(me, 2)

    def device(i, l):
        i, l = lax.rem(i, SIDE), lax.rem(l, SIDE)
        return ((l // 2) * (2 * SIDE) + i * 2 + lax.rem(l, 2),)

    def step_of(slot):
        odd = lax.rem(slot, 2)
        return odd * slot + (1 - odd) * (SIDE - slot)

    barrier = pltpu.get_barrier_semaphore()

    def greet(k, _):
        pl.semaphore_signal(barrier, inc=1, device_id=device(down + k, across), device_id_type=MESH)
        pl.semaphore_signal(barrier, inc=1, device_id=device(down, across + k), device_id_type=MESH)
        return 0

    lax.fori_loop(1, SIDE, greet, 0)

    line = lax.broadcasted_iota(jnp.int32, (SIDE, 256), 0)
    ratio = jnp.ones((SIDE, 256), F32)
    for f in range(11):
        ratio = jnp.where(line == f, scales_ref[f], ratio)
    cols[0, 0:16, :] = dir_ref[...]
    cols[0, 16:32, :] = jnp.zeros((16, 256), F32)
    cols[0, 16:27, :] = points_ref[...]
    feats = cols[0, 16:32, :] * (SCALE / ratio)
    norm = jnp.sum(feats * feats, axis=0, keepdims=True)
    block = jnp.where(line == 11, norm, jnp.where(line == 12, 1.0, feats))
    cols[0, 16:32, :] = block
    rows[0, 0:16, :] = dir_ref[...]
    rows[0, 16:32, :] = block

    pl.semaphore_wait(barrier, 2 * (SIDE - 1))

    def copy_row(s):
        return pltpu.make_async_remote_copy(
            src_ref=cols.at[0], dst_ref=rows.at[s], send_sem=row_send.at[s], recv_sem=row_recv.at[s],
            device_id=device(down, across + SIDE - step_of(s)), device_id_type=MESH)

    def copy_col(y):
        return pltpu.make_async_remote_copy(
            src_ref=cols.at[0], dst_ref=cols.at[y], send_sem=col_send.at[y], recv_sem=col_recv.at[y],
            device_id=device(down + SIDE - y, across), device_id_type=MESH)

    def go(make):
        def body(k, _):
            make(k).start()
            return 0
        return body

    def sent(make):
        def body(k, _):
            make(k).wait_send()
            return 0
        return body

    lax.fori_loop(1, SLOTS, go(copy_row), 0)
    lax.fori_loop(1, SIDE, go(copy_col), 0)

    acc_row[...] = jnp.zeros_like(acc_row)
    acc_col[...] = jnp.zeros_like(acc_col)
    square[...] = jnp.full_like(square, 1e6)
    high[...] = jnp.zeros_like(high)
    low[...] = jnp.zeros_like(low)

    def prep_row(s):
        dir_row[s] = jnp.concatenate(two(rows[s, 0:16, :]), axis=0)
        value = rows[s, 16:32, :]
        norm = jnp.sum(jnp.where(line == 11, value, 0.0), axis=0, keepdims=True)
        value = jnp.where(line == 11, 1.0, jnp.where(line == 12, norm, -2.0 * value))
        h, m, l = three(value)
        nil = jnp.zeros((SIDE, 256), F32)
        tall = jnp.concatenate([h, h, m, h, l, m, nil, nil], axis=0)
        left[s] = jnp.transpose(tall).astype(BF16)

    def prep_col(y):
        dir_col[y] = jnp.concatenate(two(cols[y, 0:16, :]), axis=0)
        h, m, l = three(cols[y, 16:32, :])
        nil = jnp.zeros((SIDE, 256), F32)
        right[y] = jnp.concatenate([h, m, h, l, h, m, nil, nil], axis=0).astype(BF16)

    prep_row(0)
    prep_col(0)

    def take_row(s, _):
        copy_row(s).wait_recv()
        prep_row(s)
        return 0

    def take_col(y, _):
        copy_col(y).wait_recv()
        prep_col(y)
        return 0

    lax.fori_loop(1, SLOTS, take_row, 0)
    lax.fori_loop(1, SIDE, take_col, 0)

    def places(t):
        g, pair = t // 8, lax.rem(t, 8)
        upper = pair // 4
        first = g * 4 + (1 - g) * upper * 8
        slots = [first, g * 4 + 1, g * 4 + 2, g * 4 + 3]
        ys = [pair * 2, pair * 2 + 1]
        ys0 = [y - (1 - g) * upper * 8 for y in ys]
        return g, slots, ys, ys0

    def dot(a, b):
        return jnp.dot(a, b, preferred_element_type=F32)

    def dot_t(a, b):
        return lax.dot_general(a, b, LAST, preferred_element_type=F32)

    def distance(s, y):
        return dot(left[s], right[y])

    def step(t, _):
        g, slots, ys, ys0 = places(jnp.maximum(t - 2, 0))
        _, slots_n, ys_n, ys0_n = places(jnp.minimum(t, 15))
        one_way = jnp.where((g == 0) & (ys0[0] == 0), 0.0, 1.0).astype(F32)
        side_sum = [None, None]
        for n in range(4):
            mine = None
            for j in range(2):
                k = n * 2 + j
                hi, lo = high[k], low[k]
                y = ys0[j] if n == 0 else ys[j]
                term = dot_t(dir_col[y], hi) + dot_t(dir_col[y], lo)
                mine = term if mine is None else mine + term
                drow = dir_row[slots[n]]
                term = dot(drow, hi) + dot(drow, lo)
                if n == 0:
                    if j == 0:
                        term = term * one_way
                    acc_col[y] += term
                else:
                    side_sum[j] = term if side_sum[j] is None else side_sum[j] + term
                hi, lo = two(matern(square[k]))
                high[k] = hi
                low[k] = lo
                y = ys0_n[j] if n == 0 else ys_n[j]
                square[k] = distance(slots_n[n], y)
            acc_row[slots[n]] += mine
        for j in range(2):
            acc_col[ys[j]] += side_sum[j]
        return 0

    lax.fori_loop(0, 18, step, 0)

    for s in (0, 8):
        hi, lo = two(matern(distance(s, 8)))
        acc_row[s] += dot_t(dir_col[8], hi) + dot_t(dir_col[8], lo)

    def give_row(s):
        return pltpu.make_async_remote_copy(
            src_ref=out_row.at[s], dst_ref=in_row.at[s], send_sem=rs_row_send.at[s], recv_sem=rs_row_recv.at[s],
            device_id=device(down, across + step_of(s)), device_id_type=MESH)

    def give_col(y):
        return pltpu.make_async_remote_copy(
            src_ref=out_col.at[y], dst_ref=in_col.at[y], send_sem=rs_col_send.at[y], recv_sem=rs_col_recv.at[y],
            device_id=device(down + y, across), device_id_type=MESH)

    def push_row(s, _):
        out_row[s] = acc_row[s, 0:16, :] + acc_row[s, 16:32, :]
        give_row(s).start()
        return 0

    def push_col(y, _):
        out_col[y] = acc_col[y, 0:16, :] + acc_col[y, 16:32, :]
        give_col(y).start()
        return 0

    lax.fori_loop(1, SLOTS, push_row, 0)
    lax.fori_loop(1, SIDE, push_col, 0)
    own = acc_row[0, 0:16, :] + acc_row[0, 16:32, :] + acc_col[0, 0:16, :] + acc_col[0, 16:32, :]

    def pull_row(s, total):
        give_row(s).wait_recv()
        return total + in_row[s]

    def pull_col(y, total):
        give_col(y).wait_recv()
        return total + in_col[y]

    own = lax.fori_loop(1, SLOTS, pull_row, own)
    own = lax.fori_loop(1, SIDE, pull_col, own)
    direction = dir_ref[...]
    residual = res_ref[...]
    image = CURVE * own + noise_ref[0] * direction

    def total(value):
        return jnp.sum(value, axis=1, keepdims=True)

    lane = lax.broadcasted_iota(jnp.int32, (16, 128), 1)
    stats = jnp.where(lane == 0, total(residual * residual), jnp.where(
        lane == 1, total(direction * image), jnp.where(
            lane == 2, total(residual * image), jnp.where(lane == 3, total(image * image), 0.0))))
    stat_col[0] = stats

    def tell_col(y):
        return pltpu.make_async_remote_copy(
            src_ref=stat_col.at[0], dst_ref=stat_col.at[y], send_sem=sc_send.at[y], recv_sem=sc_recv.at[y],
            device_id=device(down + y, across), device_id_type=MESH)

    def tell_row(x):
        return pltpu.make_async_remote_copy(
            src_ref=stat_row.at[0], dst_ref=stat_row.at[x], send_sem=sr_send.at[x], recv_sem=sr_recv.at[x],
            device_id=device(down, across + x), device_id_type=MESH)

    def hear_col(y, value):
        tell_col(y).wait_recv()
        return value + stat_col[y]

    def hear_row(x, value):
        tell_row(x).wait_recv()
        return value + stat_row[x]

    lax.fori_loop(1, SIDE, go(tell_col), 0)
    stats = lax.fori_loop(1, SIDE, hear_col, stats)
    stat_row[0] = stats
    lax.fori_loop(1, SIDE, go(tell_row), 0)
    stats = lax.fori_loop(1, SIDE, hear_row, stats)

    def pick(k):
        return jnp.sum(jnp.where(lane == k, stats, 0.0), axis=1, keepdims=True)

    rr, pap, cross, squared = pick(0), pick(1), pick(2), pick(3)
    alpha = rr / pap
    rr_next = jnp.maximum(rr - alpha * (2.0 * cross - alpha * squared), 0.0)
    res_next = residual - alpha * image
    sol_out[...] = sol_ref[...] + alpha * direction
    res_out[...] = res_next
    dir_out[...] = res_next + (rr_next / rr) * direction

    lax.fori_loop(1, SLOTS, sent(copy_row), 0)
    lax.fori_loop(1, SIDE, sent(copy_col), 0)
    lax.fori_loop(1, SLOTS, sent(give_row), 0)
    lax.fori_loop(1, SIDE, sent(give_col), 0)
    lax.fori_loop(1, SIDE, sent(tell_col), 0)
    lax.fori_loop(1, SIDE, sent(tell_row), 0)


def on_device(points, lengthscales, noise, solution, residual, direction):
    vmem = pl.BlockSpec(memory_space=pltpu.VMEM)
    smem = pl.BlockSpec(memory_space=pltpu.SMEM)
    out = jax.ShapeDtypeStruct((16, 256), F32)
    dma = pltpu.SemaphoreType.DMA
    return pl.pallas_call(
        kernel,
        out_shape=(out, out, out),
        in_specs=[smem, smem, vmem, vmem, vmem, vmem],
        out_specs=(vmem, vmem, vmem),
        scratch_shapes=[
            pltpu.VMEM((SLOTS, 32, 256), F32), pltpu.VMEM((SIDE, 32, 256), F32),
            pltpu.VMEM((SLOTS, 256, 128), BF16), pltpu.VMEM((SIDE, 128, 256), BF16),
            pltpu.VMEM((SLOTS, 32, 256), BF16), pltpu.VMEM((SIDE, 32, 256), BF16),
            pltpu.VMEM((SLOTS, 32, 256), F32), pltpu.VMEM((SIDE, 32, 256), F32),
            pltpu.VMEM((8, 256, 256), F32), pltpu.VMEM((8, 256, 256), BF16), pltpu.VMEM((8, 256, 256), BF16),
            pltpu.VMEM((SLOTS, 16, 256), F32), pltpu.VMEM((SIDE, 16, 256), F32),
            pltpu.VMEM((SLOTS, 16, 256), F32), pltpu.VMEM((SIDE, 16, 256), F32),
            pltpu.VMEM((SIDE, 16, 128), F32), pltpu.VMEM((SIDE, 16, 128), F32),
            dma((SLOTS,)), dma((SLOTS,)), dma((SIDE,)), dma((SIDE,)),
            dma((SLOTS,)), dma((SLOTS,)), dma((SIDE,)), dma((SIDE,)),
            dma((SIDE,)), dma((SIDE,)), dma((SIDE,)), dma((SIDE,)),
        ],
        compiler_params=pltpu.CompilerParams(
            collective_id=0, has_side_effects=True, vmem_limit_bytes=48 * 2**20),
    )(lengthscales, noise, points, solution, residual, direction)


def solution(mesh):
    placed = (P(None, "blk"), P(), P(), P(None, "blk"), P(None, "blk"), P(None, "blk"))
    return jax.shard_map(
        on_device,
        mesh=mesh,
        in_specs=placed,
        out_specs=(P(None, "blk"), P(None, "blk"), P(None, "blk")),
        check_vma=False,
    )
```

time: 461 us -> 67.8 us (0.15)
  blocking collectives: 149 us -> 0 us
  other arithmetic: 124 us -> 0 us
  waiting for transfers between devices: 114 us -> 0 us
  Pallas kernels: 0 us -> 61.3 us
  matrix products: 56.5 us -> 0 us
  between operations: 14.7 us -> 1.33 us
    psum x2 -> x0, blocking collectives: 149 us -> none  [the longest x1 77.1 us: on_device(): norm_now = lax.psum(jnp.sum(residual * residual, axis=1), 'blk')]
    reduce_sum x3 -> x0, other arithmetic: 120 us -> none  [the longest x1 119 us: on_device(): curv = lax.psum(jnp.sum(direction * image, axis=1), 'blk')]
    all_gather x2 -> x0, waiting for transfers between devices: 112 us -> none  [the longest x1 112 us: on_device(): lax.all_gather(points, 'blk', axis=1, tiled=True)]
    pallas_call x0 -> x1, Pallas kernels: none -> 61.3 us  [on_device(): pl.pallas_call(kernel, out_shape=(out, out, out), in_specs=[smem, smem, v...]
    dot_general x1 -> x0, matrix products: 56.5 us -> none  [apply_rows(): lax.dot_general(vectors, tile, (((1,), (1,)), ((), ())), precision=lax.Pr...]
    unnamed x8 -> x13, local copies, waits for them, and re-layouts: 0.02 us -> 4.68 us
  transfers between devices with their start and end apart: 2 -> 0, of which waited for: 1 -> 0; matrix products, arithmetic and copies ran while one was open for 27% -> 0% of each run, Pallas kernels for 0% -> 0%
where the time goes in v1:
time: 67.8 us; the launch traced here: 67.3 us
  Pallas kernels  61.3 us (90%)
  local copies, waits for them, and re-layouts  4.68 us (7%)
  between operations  1.33 us (2%)
    pallas_call x1, Pallas kernels, on_device(): pl.pallas_call(kernel, out_shape=(out, out, out), in_specs=[smem, smem, v...  61.3 us
    unnamed x13, local copies, waits for them, and re-layouts  4.68 us

profile of v1, /device:TPU:1, one launch (start us, length us, event | category | flops | bytes accessed | tf_op | source)
XLA Modules:
  0.0 67.3 jit_solution(16436546084899161854)
XLA Ops:
  0.6 0.0 copy-start.4
  1.3 0.0 copy-done.4
  1.3 0.0 copy-start
  1.3 0.7 %copy-done = f32[11,256]{1,0:T(8,128)S(1)} copy-done((f32[11,256]{1,0:T(8,128)S(1)}, f32[11,256]{1,0:T(8,128)}, u32[]{:S(2)}) %copy-start) | copy-done | bytes 11288
  2.0 0.0 copy-start.1
  2.0 0.7 %copy-done.1 = f32[16,256]{1,0:T(8,128)S(1)} copy-done((f32[16,256]{1,0:T(8,128)S(1)}, f32[16,256]{1,0:T(8,128)}, u32[]{:S(2)}) %copy-start.1) | copy-done | bytes 16408
  2.7 0.0 copy-start.2
  2.7 0.7 %copy-done.2 = f32[16,256]{1,0:T(8,128)S(1)} copy-done((f32[16,256]{1,0:T(8,128)S(1)}, f32[16,256]{1,0:T(8,128)}, u32[]{:S(2)}) %copy-start.2) | copy-done | bytes 16408
  3.5 0.0 copy-start.3
  3.5 0.7 %copy-done.3 = f32[16,256]{1,0:T(8,128)S(1)} copy-done((f32[16,256]{1,0:T(8,128)S(1)}, f32[16,256]{1,0:T(8,128)}, u32[]{:S(2)}) %copy-start.3) | copy-done | bytes 16408
  4.2 61.3 %shard_map.85 = (f32[16,256]{1,0:T(8,128)S(1)}, f32[16,256]{1,0:T(8,128)S(1)}, f32[16,256]{1,0:T(8,128)S(1)}) custom-call(f32[11]{0:T(128)S(1)} %copy-done.4, f32[1]{0:T(128)S(6)} %copy.12.noise_ref, f32[11,256]{1,0:T(8,128)S(1)} %copy-done, f32[16,256]{1,0:T(8,128)S(1)} %copy-done.1, f32[16,256]{1,0:T(8,128)S(1)} %copy-done.2, f32[16,256]{1,0:T(8,128)S(1)} %copy-done.3), custom_call_target="tpu_custom_call" | custom-call | tf_op jit(solution)/shard_map/pallas_call | solution.py:298
  65.5 0.6 copy.13
  66.1 0.6 copy.14
  66.7 0.6 copy.15
Async XLA Ops:
  0.6 0.7 copy-start.4
  1.3 0.7 %copy-start = (f32[11,256]{1,0:T(8,128)S(1)}, f32[11,256]{1,0:T(8,128)}, u32[]{:S(2)}) copy-start(f32[11,256]{1,0:T(8,128)} %points_ref.1) | copy-start | bytes 33796
  2.0 0.7 %copy-start.1 = (f32[16,256]{1,0:T(8,128)S(1)}, f32[16,256]{1,0:T(8,128)}, u32[]{:S(2)}) copy-start(f32[16,256]{1,0:T(8,128)} %sol_ref.1) | copy-start | bytes 49156
  2.7 0.7 %copy-start.2 = (f32[16,256]{1,0:T(8,128)S(1)}, f32[16,256]{1,0:T(8,128)}, u32[]{:S(2)}) copy-start(f32[16,256]{1,0:T(8,128)} %res_ref.1) | copy-start | bytes 49156
  3.5 0.7 %copy-start.3 = (f32[16,256]{1,0:T(8,128)S(1)}, f32[16,256]{1,0:T(8,128)}, u32[]{:S(2)}) copy-start(f32[16,256]{1,0:T(8,128)} %dir_ref.1) | copy-start | bytes 49156

commit v2 on v1

--- a/solution.py
+++ b/solution.py
@@ -38,10 +38,11 @@
 
 
 def kernel(
+    scales_hbm, noise_hbm, points_hbm, sol_hbm, res_hbm, dir_hbm,
+    sol_out, res_out, dir_out,
     scales_ref, noise_ref, points_ref, sol_ref, res_ref, dir_ref,
-    sol_out, res_out, dir_out,
     rows, cols, left, right, dir_row, dir_col, acc_row, acc_col, square, high, low,
-    out_row, out_col, in_row, in_col, stat_col, stat_row,
+    out_row, out_col, in_row, in_col, stat_col, stat_row, load_sem,
     row_send, row_recv, col_send, col_recv, rs_row_send, rs_row_recv, rs_col_send, rs_col_recv,
     sc_send, sc_recv, sr_send, sr_recv,
 ):
@@ -57,6 +58,14 @@
         odd = lax.rem(slot, 2)
         return odd * slot + (1 - odd) * (SIDE - slot)
 
+    loads = [
+        pltpu.make_async_copy(a, b, load_sem.at[k])
+        for k, (a, b) in enumerate((
+            (points_hbm, points_ref), (scales_hbm, scales_ref), (dir_hbm, dir_ref),
+            (noise_hbm, noise_ref), (sol_hbm, sol_ref), (res_hbm, res_ref)))
+    ]
+    for load in loads:
+        load.start()
     barrier = pltpu.get_barrier_semaphore()
 
     def greet(k, _):
@@ -65,6 +74,11 @@
         return 0
 
     lax.fori_loop(1, SIDE, greet, 0)
+
+    acc_row[...] = jnp.zeros_like(acc_row)
+    acc_col[...] = jnp.zeros_like(acc_col)
+    for load in loads:
+        load.wait()
 
     line = lax.broadcasted_iota(jnp.int32, (SIDE, 256), 0)
     ratio = jnp.ones((SIDE, 256), F32)
@@ -104,14 +118,12 @@
             return 0
         return body
 
-    lax.fori_loop(1, SLOTS, go(copy_row), 0)
-    lax.fori_loop(1, SIDE, go(copy_col), 0)
-
-    acc_row[...] = jnp.zeros_like(acc_row)
-    acc_col[...] = jnp.zeros_like(acc_col)
-    square[...] = jnp.full_like(square, 1e6)
-    high[...] = jnp.zeros_like(high)
-    low[...] = jnp.zeros_like(low)
+    lax.fori_loop(1, 4, go(copy_row), 0)
+    lax.fori_loop(1, 6, go(copy_col), 0)
+    copy_row(8).start()
+    lax.fori_loop(6, SIDE, go(copy_col), 0)
+    lax.fori_loop(4, 8, go(copy_row), 0)
+
 
     def prep_row(s):
         dir_row[s] = jnp.concatenate(two(rows[s, 0:16, :]), axis=0)
@@ -132,18 +144,13 @@
     prep_row(0)
     prep_col(0)
 
-    def take_row(s, _):
+    def take_row(s):
         copy_row(s).wait_recv()
         prep_row(s)
-        return 0
-
-    def take_col(y, _):
+
+    def take_col(y):
         copy_col(y).wait_recv()
         prep_col(y)
-        return 0
-
-    lax.fori_loop(1, SLOTS, take_row, 0)
-    lax.fori_loop(1, SIDE, take_col, 0)
 
     def places(t):
         g, pair = t // 8, lax.rem(t, 8)
@@ -163,51 +170,52 @@
     def distance(s, y):
         return dot(left[s], right[y])
 
-    def step(t, _):
-        g, slots, ys, ys0 = places(jnp.maximum(t - 2, 0))
-        _, slots_n, ys_n, ys0_n = places(jnp.minimum(t, 15))
+    def work(t, apply, entries, distances, extra=()):
+        g, slots, ys, ys0 = places(t - 2)
+        _, slots_n, ys_n, ys0_n = places(t)
         one_way = jnp.where((g == 0) & (ys0[0] == 0), 0.0, 1.0).astype(F32)
         side_sum = [None, None]
+        for s in extra:
+            hi, lo = two(matern(distance(s, 8)))
+            acc_row[s] += dot_t(dir_col[8], hi) + dot_t(dir_col[8], lo)
         for n in range(4):
             mine = None
             for j in range(2):
                 k = n * 2 + j
-                hi, lo = high[k], low[k]
-                y = ys0[j] if n == 0 else ys[j]
-                term = dot_t(dir_col[y], hi) + dot_t(dir_col[y], lo)
-                mine = term if mine is None else mine + term
-                drow = dir_row[slots[n]]
-                term = dot(drow, hi) + dot(drow, lo)
-                if n == 0:
-                    if j == 0:
-                        term = term * one_way
-                    acc_col[y] += term
-                else:
-                    side_sum[j] = term if side_sum[j] is None else side_sum[j] + term
-                hi, lo = two(matern(square[k]))
-                high[k] = hi
-                low[k] = lo
-                y = ys0_n[j] if n == 0 else ys_n[j]
-                square[k] = distance(slots_n[n], y)
-            acc_row[slots[n]] += mine
-        for j in range(2):
-            acc_col[ys[j]] += side_sum[j]
-        return 0
-
-    lax.fori_loop(0, 18, step, 0)
-
-    for s in (0, 8):
-        hi, lo = two(matern(distance(s, 8)))
-        acc_row[s] += dot_t(dir_col[8], hi) + dot_t(dir_col[8], lo)
+                if apply:
+                    hi, lo = high[k], low[k]
+                    y = ys0[j] if n == 0 else ys[j]
+                    term = dot_t(dir_col[y], hi) + dot_t(dir_col[y], lo)
+                    mine = term if mine is None else mine + term
+                    drow = dir_row[slots[n]]
+                    term = dot(drow, hi) + dot(drow, lo)
+                    if n == 0:
+                        if j == 0:
+                            term = term * one_way
+                        acc_col[y] += term
+                    else:
+                        side_sum[j] = term if side_sum[j] is None else side_sum[j] + term
+                if entries:
+                    hi, lo = two(matern(square[k]))
+                    high[k] = hi
+                    low[k] = lo
+                if distances:
+                    y = ys0_n[j] if n == 0 else ys_n[j]
+                    square[k] = distance(slots_n[n], y)
+            if apply:
+                acc_row[slots[n]] += mine
+        if apply:
+            for j in range(2):
+                acc_col[ys[j]] += side_sum[j]
 
     def give_row(s):
         return pltpu.make_async_remote_copy(
-            src_ref=out_row.at[s], dst_ref=in_row.at[s], send_sem=rs_row_send.at[s], recv_sem=rs_row_recv.at[s],
+            src_ref=out_row.at[s], dst_ref=in_row.at[s], send_sem=rs_row_send, recv_sem=rs_row_recv,
             device_id=device(down, across + step_of(s)), device_id_type=MESH)
 
     def give_col(y):
         return pltpu.make_async_remote_copy(
-            src_ref=out_col.at[y], dst_ref=in_col.at[y], send_sem=rs_col_send.at[y], recv_sem=rs_col_recv.at[y],
+            src_ref=out_col.at[y], dst_ref=in_col.at[y], send_sem=rs_col_send, recv_sem=rs_col_recv,
             device_id=device(down + y, across), device_id_type=MESH)
 
     def push_row(s, _):
@@ -220,20 +228,66 @@
         give_col(y).start()
         return 0
 
-    lax.fori_loop(1, SLOTS, push_row, 0)
-    lax.fori_loop(1, SIDE, push_col, 0)
+    take_row(1)
+    take_row(2)
+    take_row(3)
+    take_col(1)
+    work(0, False, False, True)
+    take_col(2)
+    take_col(3)
+    work(1, False, True, True)
+    take_col(4)
+    take_col(5)
+
+    def early(t, _):
+        s = jnp.where(t == 2, 8, t + 1)
+        copy_row(s).wait_recv()
+        copy_col(2 * t + 2).wait_recv()
+        copy_col(2 * t + 3).wait_recv()
+        prep_row(s)
+        prep_col(2 * t + 2)
+        prep_col(2 * t + 3)
+        work(t, True, True, True)
+        return 0
+
+    def middle(t, _):
+        work(t, True, True, True)
+        return 0
+
+    def late(t, _):
+        push_col(2 * t - 22, 0)
+        push_col(2 * t - 21, 0)
+        work(t, True, True, True)
+        return 0
+
+    lax.fori_loop(2, 7, early, 0)
+    lax.fori_loop(7, 11, middle, 0)
+    lax.fori_loop(1, 4, push_row, 0)
+    push_col(1, 0)
+    work(11, True, True, True)
+    lax.fori_loop(12, 16, late, 0)
+    push_col(10, 0)
+    push_col(11, 0)
+    work(16, True, True, False, (0, 8))
+    push_row(8, 0)
+    push_col(12, 0)
+    push_col(13, 0)
+    work(17, True, False, False)
+    push_col(14, 0)
+    push_col(15, 0)
+    lax.fori_loop(4, 8, push_row, 0)
     own = acc_row[0, 0:16, :] + acc_row[0, 16:32, :] + acc_col[0, 0:16, :] + acc_col[0, 16:32, :]
 
-    def pull_row(s, total):
-        give_row(s).wait_recv()
-        return total + in_row[s]
-
-    def pull_col(y, total):
-        give_col(y).wait_recv()
-        return total + in_col[y]
-
-    own = lax.fori_loop(1, SLOTS, pull_row, own)
-    own = lax.fori_loop(1, SIDE, pull_col, own)
+    def all_of(ref, sem):
+        blocks = ref.at[pl.ds(1, ref.shape[0] - 1)]
+        pltpu.make_async_copy(blocks, blocks, sem).wait()
+
+    all_of(in_col, rs_col_recv)
+    all_of(in_row, rs_row_recv)
+    for s in range(1, SLOTS):
+        own = own + in_row[s]
+    for y in range(1, SIDE):
+        own = own + in_col[y]
     direction = dir_ref[...]
     residual = res_ref[...]
     image = CURVE * own + noise_ref[0] * direction
@@ -241,38 +295,37 @@
     def total(value):
         return jnp.sum(value, axis=1, keepdims=True)
 
-    lane = lax.broadcasted_iota(jnp.int32, (16, 128), 1)
-    stats = jnp.where(lane == 0, total(residual * residual), jnp.where(
-        lane == 1, total(direction * image), jnp.where(
-            lane == 2, total(residual * image), jnp.where(lane == 3, total(image * image), 0.0))))
+    lane = lax.broadcasted_iota(jnp.int32, (8, 128), 1)
+    stats = jnp.zeros((8, 128), F32)
+    for k, value in enumerate((residual * residual, direction * image, residual * image, image * image)):
+        value = total(value)
+        stats = jnp.where(lane == k, value[0:8], jnp.where(lane == k + 4, value[8:16], stats))
     stat_col[0] = stats
 
     def tell_col(y):
         return pltpu.make_async_remote_copy(
-            src_ref=stat_col.at[0], dst_ref=stat_col.at[y], send_sem=sc_send.at[y], recv_sem=sc_recv.at[y],
+            src_ref=stat_col.at[0], dst_ref=stat_col.at[y], send_sem=sc_send, recv_sem=sc_recv,
             device_id=device(down + y, across), device_id_type=MESH)
 
     def tell_row(x):
         return pltpu.make_async_remote_copy(
-            src_ref=stat_row.at[0], dst_ref=stat_row.at[x], send_sem=sr_send.at[x], recv_sem=sr_recv.at[x],
+            src_ref=stat_row.at[0], dst_ref=stat_row.at[x], send_sem=sr_send, recv_sem=sr_recv,
             device_id=device(down, across + x), device_id_type=MESH)
 
-    def hear_col(y, value):
-        tell_col(y).wait_recv()
-        return value + stat_col[y]
-
-    def hear_row(x, value):
-        tell_row(x).wait_recv()
-        return value + stat_row[x]
-
-    lax.fori_loop(1, SIDE, go(tell_col), 0)
-    stats = lax.fori_loop(1, SIDE, hear_col, stats)
+    for y in range(1, SIDE):
+        tell_col(y).start()
+    all_of(stat_col, sc_recv)
+    for y in range(1, SIDE):
+        stats = stats + stat_col[y]
     stat_row[0] = stats
-    lax.fori_loop(1, SIDE, go(tell_row), 0)
-    stats = lax.fori_loop(1, SIDE, hear_row, stats)
+    for x in range(1, SIDE):
+        tell_row(x).start()
+    all_of(stat_row, sr_recv)
+    for x in range(1, SIDE):
+        stats = stats + stat_row[x]
 
     def pick(k):
-        return jnp.sum(jnp.where(lane == k, stats, 0.0), axis=1, keepdims=True)
+        return jnp.concatenate([total(jnp.where(lane == k + h, stats, 0.0)) for h in (0, 4)], axis=0)
 
     rr, pap, cross, squared = pick(0), pick(1), pick(2), pick(3)
     alpha = rr / pap
@@ -284,23 +337,24 @@
 
     lax.fori_loop(1, SLOTS, sent(copy_row), 0)
     lax.fori_loop(1, SIDE, sent(copy_col), 0)
-    lax.fori_loop(1, SLOTS, sent(give_row), 0)
-    lax.fori_loop(1, SIDE, sent(give_col), 0)
-    lax.fori_loop(1, SIDE, sent(tell_col), 0)
-    lax.fori_loop(1, SIDE, sent(tell_row), 0)
+    all_of(out_row, rs_row_send)
+    all_of(out_col, rs_col_send)
+    all_of(stat_col, sc_send)
+    all_of(stat_row, sr_send)
 
 
 def on_device(points, lengthscales, noise, solution, residual, direction):
     vmem = pl.BlockSpec(memory_space=pltpu.VMEM)
-    smem = pl.BlockSpec(memory_space=pltpu.SMEM)
     out = jax.ShapeDtypeStruct((16, 256), F32)
     dma = pltpu.SemaphoreType.DMA
     return pl.pallas_call(
         kernel,
         out_shape=(out, out, out),
-        in_specs=[smem, smem, vmem, vmem, vmem, vmem],
+        in_specs=[pl.BlockSpec(memory_space=pltpu.HBM)] * 6,
         out_specs=(vmem, vmem, vmem),
         scratch_shapes=[
+            pltpu.SMEM((11,), F32), pltpu.SMEM((1,), F32), pltpu.VMEM((11, 256), F32),
+            pltpu.VMEM((16, 256), F32), pltpu.VMEM((16, 256), F32), pltpu.VMEM((16, 256), F32),
             pltpu.VMEM((SLOTS, 32, 256), F32), pltpu.VMEM((SIDE, 32, 256), F32),
             pltpu.VMEM((SLOTS, 256, 128), BF16), pltpu.VMEM((SIDE, 128, 256), BF16),
             pltpu.VMEM((SLOTS, 32, 256), BF16), pltpu.VMEM((SIDE, 32, 256), BF16),
@@ -308,10 +362,9 @@
             pltpu.VMEM((8, 256, 256), F32), pltpu.VMEM((8, 256, 256), BF16), pltpu.VMEM((8, 256, 256), BF16),
             pltpu.VMEM((SLOTS, 16, 256), F32), pltpu.VMEM((SIDE, 16, 256), F32),
             pltpu.VMEM((SLOTS, 16, 256), F32), pltpu.VMEM((SIDE, 16, 256), F32),
-            pltpu.VMEM((SIDE, 16, 128), F32), pltpu.VMEM((SIDE, 16, 128), F32),
+            pltpu.VMEM((SIDE, 8, 128), F32), pltpu.VMEM((SIDE, 8, 128), F32), dma((6,)),
             dma((SLOTS,)), dma((SLOTS,)), dma((SIDE,)), dma((SIDE,)),
-            dma((SLOTS,)), dma((SLOTS,)), dma((SIDE,)), dma((SIDE,)),
-            dma((SIDE,)), dma((SIDE,)), dma((SIDE,)), dma((SIDE,)),
+            dma, dma, dma, dma, dma, dma, dma, dma,
         ],
         compiler_params=pltpu.CompilerParams(
             collective_id=0, has_side_effects=True, vmem_limit_bytes=48 * 2**20),

time: 67.8 us -> 60.8 us (0.90)
  Pallas kernels: 61.3 us -> 54.3 us
    pallas_call x1, Pallas kernels: 61.3 us -> 54.3 us  [on_device(): pl.pallas_call(kernel, out_shape=(out, out, out), in_specs=[pl.BlockSpec(...]
where the time goes in v2:
time: 60.8 us; the launch traced here: 60.3 us
  Pallas kernels  54.3 us (89%)
  local copies, waits for them, and re-layouts  4.68 us (8%)
  between operations  1.33 us (2%)
    pallas_call x1, Pallas kernels, on_device(): pl.pallas_call(kernel, out_shape=(out, out, out), in_specs=[pl.BlockSpec(...  54.3 us
    unnamed x13, local copies, waits for them, and re-layouts  4.68 us

profile of v2, /device:TPU:1, one launch (start us, length us, event | category | flops | bytes accessed | tf_op | source)
XLA Modules:
  0.0 60.3 jit_solution(16128954357320154806)
XLA Ops:
  0.6 0.0 copy-start.4
  1.3 0.0 copy-done.4
  1.3 0.0 copy-start
  1.3 0.7 %copy-done = f32[11,256]{1,0:T(8,128)S(1)} copy-done((f32[11,256]{1,0:T(8,128)S(1)}, f32[11,256]{1,0:T(8,128)}, u32[]{:S(2)}) %copy-start) | copy-done | bytes 11288
  2.0 0.0 copy-start.1
  2.0 0.7 %copy-done.1 = f32[16,256]{1,0:T(8,128)S(1)} copy-done((f32[16,256]{1,0:T(8,128)S(1)}, f32[16,256]{1,0:T(8,128)}, u32[]{:S(2)}) %copy-start.1) | copy-done | bytes 16408
  2.7 0.0 copy-start.2
  2.7 0.7 %copy-done.2 = f32[16,256]{1,0:T(8,128)S(1)} copy-done((f32[16,256]{1,0:T(8,128)S(1)}, f32[16,256]{1,0:T(8,128)}, u32[]{:S(2)}) %copy-start.2) | copy-done | bytes 16408
  3.5 0.0 copy-start.3
  3.5 0.7 %copy-done.3 = f32[16,256]{1,0:T(8,128)S(1)} copy-done((f32[16,256]{1,0:T(8,128)S(1)}, f32[16,256]{1,0:T(8,128)}, u32[]{:S(2)}) %copy-start.3) | copy-done | bytes 16408
  4.2 54.3 %shard_map.85 = (f32[16,256]{1,0:T(8,128)S(1)}, f32[16,256]{1,0:T(8,128)S(1)}, f32[16,256]{1,0:T(8,128)S(1)}) custom-call(f32[11]{0:T(128)S(1)} %copy-done.4, f32[1]{0:T(128)S(6)} %copy.12.noise_hbm, f32[11,256]{1,0:T(8,128)S(1)} %copy-done, f32[16,256]{1,0:T(8,128)S(1)} %copy-done.1, f32[16,256]{1,0:T(8,128)S(1)} %copy-done.2, f32[16,256]{1,0:T(8,128)S(1)} %copy-done.3), custom_call_target="tpu_custom_call" | custom-call | tf_op jit(solution)/shard_map/pallas_call | solution.py:350
  58.5 0.6 %copy.13 = f32[16,256]{1,0:T(8,128)} copy(f32[16,256]{1,0:T(8,128)S(1)} %get-tuple-element.6) | data formatting | bytes 32768
  59.1 0.6 %copy.14 = f32[16,256]{1,0:T(8,128)} copy(f32[16,256]{1,0:T(8,128)S(1)} %get-tuple-element.7) | data formatting | bytes 32768
  59.7 0.6 %copy.15 = f32[16,256]{1,0:T(8,128)} copy(f32[16,256]{1,0:T(8,128)S(1)} %get-tuple-element.8) | data formatting | bytes 32768
Async XLA Ops:
  0.6 0.7 %copy-start.4 = (f32[11]{0:T(128)S(1)}, f32[11]{0:T(128)}, u32[]{:S(2)}) copy-start(f32[11]{0:T(128)} %scales_hbm.1) | copy-start | bytes 136
  1.3 0.7 %copy-start = (f32[11,256]{1,0:T(8,128)S(1)}, f32[11,256]{1,0:T(8,128)}, u32[]{:S(2)}) copy-start(f32[11,256]{1,0:T(8,128)} %points_hbm.1) | copy-start | bytes 33796
  2.0 0.7 %copy-start.1 = (f32[16,256]{1,0:T(8,128)S(1)}, f32[16,256]{1,0:T(8,128)}, u32[]{:S(2)}) copy-start(f32[16,256]{1,0:T(8,128)} %sol_hbm.1) | copy-start | bytes 49156
  2.7 0.7 %copy-start.2 = (f32[16,256]{1,0:T(8,128)S(1)}, f32[16,256]{1,0:T(8,128)}, u32[]{:S(2)}) copy-start(f32[16,256]{1,0:T(8,128)} %res_hbm.1) | copy-start | bytes 49156
  3.5 0.7 %copy-start.3 = (f32[16,256]{1,0:T(8,128)S(1)}, f32[16,256]{1,0:T(8,128)}, u32[]{:S(2)}) copy-start(f32[16,256]{1,0:T(8,128)} %dir_hbm.1) | copy-start | bytes 49156

commit v3 on v2

v3 whole, which is shorter than its diff:
```python
import math

import jax
import jax.numpy as jnp
from jax import lax
from jax.experimental import pallas as pl
from jax.experimental.pallas import tpu as pltpu
from jax.sharding import PartitionSpec as P

MESH = pl.DeviceIdType.MESH
F32, BF16 = jnp.float32, jnp.bfloat16
SIDE = 16
PLACES = (4, 1, 7, 5, 12, 15, 13, 8, 11, 14, 9, 10, 6, 2, 3, 0)
OWN = SIDE - 1
SLOTS = 9
LN2 = math.log(2.0)
SCALE = math.sqrt(5.0) / LN2
CURVE = LN2 * LN2 / 3.0
BEND = 3.0 / LN2
LIFT = 3.0 / (LN2 * LN2)
LAST = (((1,), (1,)), ((), ()))


def three(value):
    high = value.astype(BF16).astype(F32)
    rest = value - high
    middle = rest.astype(BF16).astype(F32)
    return high, middle, (rest - middle).astype(BF16).astype(F32)


def two(value):
    high = value.astype(BF16)
    return high, (value - high.astype(F32)).astype(BF16)


def matern(square):
    square = jnp.maximum(square, 1e-30)
    root = square * lax.rsqrt(square)
    return (square + BEND * root + LIFT) * jnp.exp2(-root)


def kernel(
    scales_hbm, noise_hbm, points_hbm, sol_hbm, res_hbm, dir_hbm,
    out_ref,
    scales_ref, noise_ref, points_ref, sol_ref, res_ref, dir_ref,
    rows, cols, left, right, dir_row, dir_col, acc_row, acc_col, square, high, low,
    out_row, out_col, in_row, in_col, stat_col, stat_row, load_sem,
    row_send, row_recv, col_send, col_recv, rs_row_send, rs_row_recv, rs_col_send, rs_col_recv,
    sc_send, sc_recv, sr_send, sr_recv,
):
    me = lax.axis_index("blk")
    down = lax.rem(me // 2, SIDE)
    across = (me // (2 * SIDE)) * 2 + lax.rem(me, 2)

    def device(i, l):
        i, l = lax.rem(i, SIDE), lax.rem(l, SIDE)
        return ((l // 2) * (2 * SIDE) + i * 2 + lax.rem(l, 2),)

    def step_of(slot):
        odd = lax.rem(slot, 2)
        return odd * slot + (1 - odd) * (SIDE - slot)

    loads = [
        pltpu.make_async_copy(a, b, load_sem.at[k])
        for k, (a, b) in enumerate((
            (points_hbm, points_ref), (scales_hbm, scales_ref), (dir_hbm, dir_ref),
            (noise_hbm, noise_ref), (sol_hbm, sol_ref), (res_hbm, res_ref)))
    ]
    for load in loads:
        load.start()
    def offset_of(p):
        if isinstance(p, int):
            return PLACES[p]
        offset = PLACES[0]
        for k in range(1, SIDE):
            offset = jnp.where(p == k, PLACES[k], offset)
        return offset

    barrier = pltpu.get_barrier_semaphore()

    def greet(k, _):
        pl.semaphore_signal(barrier, inc=1, device_id=device(down + k, across), device_id_type=MESH)
        pl.semaphore_signal(barrier, inc=1, device_id=device(down, across + k), device_id_type=MESH)
        return 0

    lax.fori_loop(1, SIDE, greet, 0)

    acc_row[...] = jnp.zeros_like(acc_row)
    acc_col[...] = jnp.zeros_like(acc_col)
    for load in loads:
        load.wait()

    line = lax.broadcasted_iota(jnp.int32, (SIDE, 256), 0)
    ratio = jnp.ones((SIDE, 256), F32)
    for f in range(11):
        ratio = jnp.where(line == f, scales_ref[f], ratio)
    cols[OWN, 0:16, :] = dir_ref[...]
    cols[OWN, 16:32, :] = jnp.zeros((16, 256), F32)
    cols[OWN, 16:27, :] = points_ref[...]
    feats = cols[OWN, 16:32, :] * (SCALE / ratio)
    norm = jnp.sum(feats * feats, axis=0, keepdims=True)
    block = jnp.where(line == 11, norm, jnp.where(line == 12, 1.0, feats))
    cols[OWN, 16:32, :] = block
    rows[0, 0:16, :] = dir_ref[...]
    rows[0, 16:32, :] = block

    pl.semaphore_wait(barrier, 2 * (SIDE - 1))

    def copy_row(s):
        return pltpu.make_async_remote_copy(
            src_ref=cols.at[OWN], dst_ref=rows.at[s], send_sem=row_send, recv_sem=row_recv.at[s],
            device_id=device(down, across + SIDE - step_of(s)), device_id_type=MESH)

    def copy_col(p):
        return pltpu.make_async_remote_copy(
            src_ref=cols.at[OWN], dst_ref=cols.at[p], send_sem=col_send, recv_sem=col_recv.at[p],
            device_id=device(down + SIDE - offset_of(p), across), device_id_type=MESH)

    def arrived(ref, sem):
        pltpu.make_async_copy(ref, ref, sem).wait()

    for s in (1, 2, 3):
        copy_row(s).start()
    for p in range(0, 4):
        copy_col(p).start()
    copy_row(8).start()
    for p in range(4, 8):
        copy_col(p).start()
    for s in (4, 5, 6, 7):
        copy_row(s).start()
    for p in range(8, OWN):
        copy_col(p).start()

    def prep_row(s):
        dir_row[s] = jnp.concatenate(two(rows[s, 0:16, :]), axis=0)
        value = rows[s, 16:32, :]
        norm = jnp.sum(jnp.where(line == 11, value, 0.0), axis=0, keepdims=True)
        value = jnp.where(line == 11, 1.0, jnp.where(line == 12, norm, -2.0 * value))
        h, m, l = three(value)
        nil = jnp.zeros((SIDE, 256), F32)
        tall = jnp.concatenate([h, h, m, h, l, m, nil, nil], axis=0)
        left[s] = jnp.transpose(tall).astype(BF16)

    def prep_col(y):
        dir_col[y] = jnp.concatenate(two(cols[y, 0:16, :]), axis=0)
        h, m, l = three(cols[y, 16:32, :])
        nil = jnp.zeros((SIDE, 256), F32)
        right[y] = jnp.concatenate([h, m, h, l, h, m, nil, nil], axis=0).astype(BF16)

    prep_row(0)
    prep_col(OWN)

    def take_row(s):
        arrived(rows.at[s], row_recv.at[s])
        prep_row(s)

    def take_col(p):
        arrived(cols.at[p], col_recv.at[p])
        prep_col(p)

    def places(t):
        near = jnp.where((t < 4) | (t >= 12), 1, 0)
        pair = jnp.where(t < 4, t, jnp.where(t < 12, t - 4, t - 8))
        first = jnp.where(near == 0, 4, jnp.where((pair >= 2) & (pair <= 5), 8, 0))
        base = 4 * (1 - near)
        return near, pair, [first, base + 1, base + 2, base + 3]

    def dot(a, b):
        return jnp.dot(a, b, preferred_element_type=F32)

    def dot_t(a, b):
        return lax.dot_general(a, b, LAST, preferred_element_type=F32)

    def distance(s, y):
        return dot(left[s], right[y])

    def spread(d, hi, lo, product):
        both, rest = product(d, hi), product(d[0:16], lo)
        return jnp.concatenate([both[0:16] + rest, both[16:32]], axis=0)

    def leftover(s, p):
        hi, lo = two(matern(distance(s, p)))
        acc_row[s] += spread(dir_col[p], hi, lo, dot_t)

    def work(t, apply, entries, distances):
        near, pair, slots = places(t - 2)
        _, pair_n, slots_n = places(t)
        one_way = jnp.where((near == 1) & ((pair == 3) | (pair == 7)), 0.0, 1.0).astype(F32)
        side_sum = [None, None]
        for n in range(4):
            mine = None
            for j in range(2):
                k = n * 2 + j
                if apply:
                    hi, lo = high[k], low[k]
                    term = spread(dir_col[pair * 2 + j], hi, lo, dot_t)
                    mine = term if mine is None else mine + term
                    term = spread(dir_row[slots[n]], hi, lo, dot)
                    if n == 0 and j == 1:
                        term = term * one_way
                    side_sum[j] = term if side_sum[j] is None else side_sum[j] + term
                if entries:
                    hi, lo = two(matern(square[k]))
                    high[k] = hi
                    low[k] = lo
                if distances:
                    square[k] = distance(slots_n[n], pair_n * 2 + j)
            if apply:
                acc_row[slots[n]] += mine
        if apply:
            for j in range(2):
                acc_col[pair * 2 + j] += side_sum[j]

    def give_row(s):
        return pltpu.make_async_remote_copy(
            src_ref=out_row.at[s], dst_ref=in_row.at[s], send_sem=rs_row_send, recv_sem=rs_row_recv,
            device_id=device(down, across + step_of(s)), device_id_type=MESH)

    def give_col(p):
        return pltpu.make_async_remote_copy(
            src_ref=out_col.at[p], dst_ref=in_col.at[p], send_sem=rs_col_send, recv_sem=rs_col_recv,
            device_id=device(down + offset_of(p), across), device_id_type=MESH)

    def push_row(s):
        out_row[s] = acc_row[s, 0:16, :] + acc_row[s, 16:32, :]
        give_row(s).start()

    def push_col(p):
        out_col[p] = acc_col[p, 0:16, :] + acc_col[p, 16:32, :]
        give_col(p).start()

    take_row(1)
    take_row(2)
    take_row(3)
    take_col(0)
    take_col(1)
    work(0, False, False, True)
    take_col(2)
    take_col(3)
    work(1, False, True, True)

    def early(t, _):
        @pl.when(t == 2)
        def _():
            take_row(8)

        @pl.when(t == 3)
        def _():
            for s in (4, 5, 6, 7):
                arrived(rows.at[s], row_recv.at[s])
            for s in (4, 5, 6, 7):
                prep_row(s)

        for j in range(2):
            arrived(cols.at[2 * t + j], col_recv.at[2 * t + j])
        for j in range(2):
            prep_col(2 * t + j)
        work(t, True, True, True)
        return 0

    def late(t, _):
        @pl.when((t <= 10) | (t == 15))
        def _():
            p = jnp.where(t == 15, 8, 2 * t - 14)
            push_col(p)
            push_col(p + 1)

        @pl.when(t == 14)
        def _():
            for s in (4, 5, 6, 7):
                push_row(s)

        work(t, True, True, True)
        return 0

    lax.fori_loop(2, 7, early, 0)
    arrived(cols.at[14], col_recv.at[14])
    prep_col(14)
    leftover(0, 7)
    leftover(8, OWN)
    lax.fori_loop(7, 16, late, 0)
    push_col(10)
    push_col(11)
    push_row(8)
    work(16, True, True, False)
    push_col(12)
    push_col(13)
    work(17, True, False, False)
    for s in (3, 2, 1):
        push_row(s)
    push_col(14)
    own = acc_row[0, 0:16, :] + acc_row[0, 16:32, :] + acc_col[OWN, 0:16, :] + acc_col[OWN, 16:32, :]

    arrived(in_col.at[pl.ds(0, SIDE - 1)], rs_col_recv)
    for p in range(SIDE - 1):
        own = own + in_col[p]
    arrived(in_row.at[pl.ds(1, SLOTS - 1)], rs_row_recv)
    for s in range(1, SLOTS):
        own = own + in_row[s]
    direction = dir_ref[...]
    residual = res_ref[...]
    image = CURVE * own + noise_ref[0] * direction

    def total(value):
        return jnp.sum(value, axis=1, keepdims=True)

    lane = lax.broadcasted_iota(jnp.int32, (8, 128), 1)
    stats = jnp.zeros((8, 128), F32)
    for k, value in enumerate((residual * residual, direction * image, residual * image, image * image)):
        value = total(value)
        stats = jnp.where(lane == k, value[0:8], jnp.where(lane == k + 4, value[8:16], stats))
    stat_col[0] = stats

    def tell_col(y):
        return pltpu.make_async_remote_copy(
            src_ref=stat_col.at[0], dst_ref=stat_col.at[y], send_sem=sc_send, recv_sem=sc_recv,
            device_id=device(down + y, across), device_id_type=MESH)

    def tell_row(x):
        return pltpu.make_async_remote_copy(
            src_ref=stat_row.at[0], dst_ref=stat_row.at[x], send_sem=sr_send, recv_sem=sr_recv,
            device_id=device(down, across + x), device_id_type=MESH)

    for y in range(1, SIDE):
        tell_col(y).start()
    arrived(stat_col.at[pl.ds(1, SIDE - 1)], sc_recv)
    for y in range(1, SIDE):
        stats = stats + stat_col[y]
    stat_row[0] = stats
    for x in range(1, SIDE):
        tell_row(x).start()
    arrived(stat_row.at[pl.ds(1, SIDE - 1)], sr_recv)
    for x in range(1, SIDE):
        stats = stats + stat_row[x]

    def pick(k):
        return jnp.concatenate([total(jnp.where(lane == k + h, stats, 0.0)) for h in (0, 4)], axis=0)

    rr, pap, cross, squared = pick(0), pick(1), pick(2), pick(3)
    alpha = rr / pap
    rr_next = jnp.maximum(rr - alpha * (2.0 * cross - alpha * squared), 0.0)
    out_ref[0:16, :] = image
    out_ref[16:32, :] = jnp.broadcast_to(alpha, (16, 256))
    out_ref[32:48, :] = jnp.broadcast_to(rr_next / rr, (16, 256))

    arrived(rows.at[pl.ds(1, SLOTS - 1)], row_send)
    arrived(cols.at[pl.ds(0, SIDE - 1)], col_send)
    arrived(out_row.at[pl.ds(1, SLOTS - 1)], rs_row_send)
    arrived(out_col.at[pl.ds(0, SIDE - 1)], rs_col_send)
    arrived(stat_col.at[pl.ds(1, SIDE - 1)], sc_send)
    arrived(stat_row.at[pl.ds(1, SIDE - 1)], sr_send)


def on_device(points, lengthscales, noise, solution, residual, direction):
    vmem = pl.BlockSpec(memory_space=pltpu.VMEM)
    out = jax.ShapeDtypeStruct((16, 256), F32)
    dma = pltpu.SemaphoreType.DMA
    packed = pl.pallas_call(
        kernel,
        out_shape=jax.ShapeDtypeStruct((48, 256), F32),
        in_specs=[pl.BlockSpec(memory_space=pltpu.HBM)] * 6,
        out_specs=vmem,
        scratch_shapes=[
            pltpu.SMEM((11,), F32), pltpu.SMEM((1,), F32), pltpu.VMEM((11, 256), F32),
            pltpu.VMEM((16, 256), F32), pltpu.VMEM((16, 256), F32), pltpu.VMEM((16, 256), F32),
            pltpu.VMEM((SLOTS, 32, 256), F32), pltpu.VMEM((SIDE, 32, 256), F32),
            pltpu.VMEM((SLOTS, 256, 128), BF16), pltpu.VMEM((SIDE, 128, 256), BF16),
            pltpu.VMEM((SLOTS, 32, 256), BF16), pltpu.VMEM((SIDE, 32, 256), BF16),
            pltpu.VMEM((SLOTS, 32, 256), F32), pltpu.VMEM((SIDE, 32, 256), F32),
            pltpu.VMEM((8, 256, 256), F32), pltpu.VMEM((8, 256, 256), BF16), pltpu.VMEM((8, 256, 256), BF16),
            pltpu.VMEM((SLOTS, 16, 256), F32), pltpu.VMEM((SIDE, 16, 256), F32),
            pltpu.VMEM((SLOTS, 16, 256), F32), pltpu.VMEM((SIDE, 16, 256), F32),
            pltpu.VMEM((SIDE, 8, 128), F32), pltpu.VMEM((SIDE, 8, 128), F32), dma((6,)),
            dma, dma((SLOTS,)), dma, dma((SIDE,)),
            dma, dma, dma, dma, dma, dma, dma, dma,
        ],
        compiler_params=pltpu.CompilerParams(
            collective_id=0, has_side_effects=True, vmem_limit_bytes=60 * 2**20),
    )(lengthscales, noise, points, solution, residual, direction)
    image, alpha, beta = packed[0:16], packed[16:32], packed[32:48]
    residual_next = residual - alpha * image
    return solution + alpha * direction, residual_next, residual_next + beta * direction


def solution(mesh):
    placed = (P(None, "blk"), P(), P(), P(None, "blk"), P(None, "blk"), P(None, "blk"))
    return jax.shard_map(
        on_device,
        mesh=mesh,
        in_specs=placed,
        out_specs=(P(None, "blk"), P(None, "blk"), P(None, "blk")),
        check_vma=False,
    )
```

time: 60.8 us -> 56.2 us (0.924)
  local copies, waits for them, and re-layouts: 4.68 us -> 0.01 us
  other arithmetic: 0 us -> 1.38 us
  Pallas kernels: 54.3 us -> 53.3 us
    unnamed x13 -> x6, local copies, waits for them, and re-layouts: 4.68 us -> 0.01 us
    add x0 -> x1, other arithmetic: none -> 1.38 us  [on_device(): residual_next + beta * direction]
    pallas_call x1, Pallas kernels: 54.3 us -> 53.3 us  [on_device(): pl.pallas_call(kernel, out_shape=jax.ShapeDtypeStruct((48, 256), F32), in...]
where the time goes in v3:
time: 56.2 us; the launch traced here: 56 us
  Pallas kernels  53.3 us (95%)
  other arithmetic  1.38 us (2%)
  between operations  1.33 us (2%)
    pallas_call x1, Pallas kernels, on_device(): pl.pallas_call(kernel, out_shape=jax.ShapeDtypeStruct((48, 256), F32), in...  53.3 us
    add x1, other arithmetic, on_device(): residual_next + beta * direction  1.38 us

profile of v3, /device:TPU:1, one launch (start us, length us, event | category | flops | bytes accessed | tf_op | source)
XLA Modules:
  0.0 56.0 jit_solution(11767337614338078627)
XLA Ops:
  1.3 0.0 copy-start
  1.3 0.0 copy-start.1
  1.3 0.0 copy-start.2
  1.3 53.3 %shard_map.85 = f32[48,256]{1,0:T(8,128)} custom-call(f32[11]{0:T(128)} %scales_hbm.1, f32[1]{0:T(128)S(6)} %copy.9.noise_hbm, f32[11,256]{1,0:T(8,128)} %points_hbm.1, f32[16,256]{1,0:T(8,128)} %sol_hbm.1, f32[16,256]{1,0:T(8,128)} %res_hbm.1, f32[16,256]{1,0:T(8,128)} %dir_hbm.1), custom_call_target="tpu_custom_call" | custom-call | tf_op jit(solution)/shard_map/pallas_call | solution.py:358
  54.6 0.0 copy-done
  54.6 0.0 copy-done.1
  54.6 0.0 copy-done.2
  54.6 1.4 %multiply_add_fusion = (f32[16,256]{1,0:T(8,128)}, f32[16,256]{1,0:T(8,128)}, f32[16,256]{1,0:T(8,128)}) fusion(f32[16,256]{1,0:T(8,128)S(1)} %copy-done, f32[48,256]{1,0:T(8,128)} %shard_map.85, f32[16,256]{1,0:T(8,128)S(1)} %copy-done.2, f32[16,256]{1,0:T(8,128)S(1)} %copy-done.1), kind=kLoop, calls=%fused_computation | loop fusion | flops 24576 | bytes 147456 | tf_op jit(solution)/shard_map/add | solution.py:382
Async XLA Ops:
  1.3 53.3 %copy-start = (f32[16,256]{1,0:T(8,128)S(1)}, f32[16,256]{1,0:T(8,128)}, u32[]{:S(2)}) copy-start(f32[16,256]{1,0:T(8,128)} %dir_hbm.1) | copy-start | bytes 49156
  1.3 53.3 %copy-start.1 = (f32[16,256]{1,0:T(8,128)S(1)}, f32[16,256]{1,0:T(8,128)}, u32[]{:S(2)}) copy-start(f32[16,256]{1,0:T(8,128)} %sol_hbm.1) | copy-start | bytes 49156
  1.3 53.3 %copy-start.2 = (f32[16,256]{1,0:T(8,128)S(1)}, f32[16,256]{1,0:T(8,128)}, u32[]{:S(2)}) copy-start(f32[16,256]{1,0:T(8,128)} %res_hbm.1) | copy-start | bytes 49156

commit v4 on v3

v4 whole, which is shorter than its diff:
```python
import math

import jax
import jax.numpy as jnp
from jax import lax
from jax.experimental import pallas as pl
from jax.experimental.pallas import tpu as pltpu
from jax.sharding import PartitionSpec as P

MESH = pl.DeviceIdType.MESH
F32, BF16 = jnp.float32, jnp.bfloat16
SIDE = 16
PLACES = (4, 1, 7, 5, 12, 15, 13, 8, 11, 14, 9, 10, 6, 2, 3, 0)
OWN = SIDE - 1
STEPS = (0, 15, 2, 13, 12, 5, 10, 7, 8)
SLOTS = 9
LN2 = math.log(2.0)
SCALE = math.sqrt(5.0) / LN2
CURVE = LN2 * LN2 / 3.0
BEND = 3.0 / LN2
LIFT = 3.0 / (LN2 * LN2)
LAST = (((1,), (1,)), ((), ()))


def three(value):
    high = value.astype(BF16).astype(F32)
    rest = value - high
    middle = rest.astype(BF16).astype(F32)
    return high, middle, (rest - middle).astype(BF16).astype(F32)


def two(value):
    high = value.astype(BF16)
    return high, (value - high.astype(F32)).astype(BF16)


def matern(square):
    square = jnp.maximum(square, 1e-30)
    root = square * lax.rsqrt(square)
    return (square + BEND * root + LIFT) * jnp.exp2(-root)


def kernel(
    scales_hbm, noise_hbm, points_hbm, sol_hbm, res_hbm, dir_hbm,
    out_ref,
    scales_ref, noise_ref, points_ref, sol_ref, res_ref, dir_ref,
    rows, cols, left, right, dir_row, dir_col, acc_row, acc_col, square, high, low,
    out_row, out_col, in_row, in_col, stat_col, stat_row, load_sem,
    row_send, row_near, row_recv, col_send, col_near, col_recv, rs_row_send, rs_row_recv, rs_col_send, rs_col_recv,
    sc_send, sc_recv, sr_send, sr_recv,
):
    me = lax.axis_index("blk")
    down = lax.rem(me // 2, SIDE)
    across = (me // (2 * SIDE)) * 2 + lax.rem(me, 2)

    def device(i, l):
        i, l = lax.rem(i, SIDE), lax.rem(l, SIDE)
        return ((l // 2) * (2 * SIDE) + i * 2 + lax.rem(l, 2),)

    def offset_of(p):
        if isinstance(p, int):
            return PLACES[p]
        offset = PLACES[0]
        for k in range(1, SIDE):
            offset = jnp.where(p == k, PLACES[k], offset)
        return offset

    barrier = pltpu.get_barrier_semaphore()

    def greet(k, _):
        pl.semaphore_signal(barrier, inc=1, device_id=device(down + k, across), device_id_type=MESH)
        pl.semaphore_signal(barrier, inc=1, device_id=device(down, across + k), device_id_type=MESH)
        return 0

    lax.fori_loop(1, SIDE, greet, 0)
    loads = [
        pltpu.make_async_copy(a, b, load_sem.at[k])
        for k, (a, b) in enumerate((
            (points_hbm, points_ref), (scales_hbm, scales_ref), (dir_hbm, dir_ref),
            (noise_hbm, noise_ref), (sol_hbm, sol_ref), (res_hbm, res_ref)))
    ]
    for load in loads:
        load.start()

    acc_row[...] = jnp.zeros_like(acc_row)
    acc_col[...] = jnp.zeros_like(acc_col)
    for load in loads:
        load.wait()

    line = lax.broadcasted_iota(jnp.int32, (SIDE, 256), 0)
    ratio = jnp.ones((SIDE, 256), F32)
    for f in range(11):
        ratio = jnp.where(line == f, scales_ref[f], ratio)
    cols[OWN, 0:16, :] = dir_ref[...]
    cols[OWN, 16:32, :] = jnp.zeros((16, 256), F32)
    cols[OWN, 16:27, :] = points_ref[...]
    feats = cols[OWN, 16:32, :] * (SCALE / ratio)
    norm = jnp.sum(feats * feats, axis=0, keepdims=True)
    block = jnp.where(line == 11, norm, jnp.where(line == 12, 1.0, feats))
    cols[OWN, 16:32, :] = block
    rows[0, 0:16, :] = dir_ref[...]
    rows[0, 16:32, :] = block

    pl.semaphore_wait(barrier, 2 * (SIDE - 1))

    FEATS, DIRS = pl.ds(16, 16), pl.ds(0, 16)

    def copy_row(s, part):
        return pltpu.make_async_remote_copy(
            src_ref=cols.at[OWN, part], dst_ref=rows.at[s, part], send_sem=row_send,
            recv_sem=(row_near if part is FEATS else row_recv).at[s],
            device_id=device(down, across + SIDE - STEPS[s]), device_id_type=MESH)

    def copy_col(p, part):
        return pltpu.make_async_remote_copy(
            src_ref=cols.at[OWN, part], dst_ref=cols.at[p, part], send_sem=col_send,
            recv_sem=(col_near if part is FEATS else col_recv).at[p],
            device_id=device(down + SIDE - offset_of(p), across), device_id_type=MESH)

    def arrived(ref, sem):
        pltpu.make_async_copy(ref, ref, sem).wait()

    def ship(*lots):
        for make, part, ids in lots:
            for k in ids:
                make(k, part).start()

    ship((copy_row, FEATS, (1, 2, 3)), (copy_col, FEATS, (0, 1, 2, 3)), (copy_row, DIRS, (1, 2, 3)), (copy_row, FEATS, (8,)), (copy_col, FEATS, (4, 5, 6, 7)), (copy_col, DIRS, (0, 1, 2, 3)), (copy_row, FEATS, (6, 7, 4, 5)), (copy_col, FEATS, (8, 9, 10, 11)), (copy_row, DIRS, (8,)), (copy_col, DIRS, (4, 5, 6, 7)),)

    def prep_row(s):
        value = rows[s, 16:32, :]
        norm = jnp.sum(jnp.where(line == 11, value, 0.0), axis=0, keepdims=True)
        value = jnp.where(line == 11, 1.0, jnp.where(line == 12, norm, -2.0 * value))
        h, m, l = three(value)
        nil = jnp.zeros((SIDE, 256), F32)
        tall = jnp.concatenate([h, h, m, h, l, m, nil, nil], axis=0)
        left[s] = jnp.transpose(tall).astype(BF16)

    def prep_col(p):
        h, m, l = three(cols[p, 16:32, :])
        nil = jnp.zeros((SIDE, 256), F32)
        right[p] = jnp.concatenate([h, m, h, l, h, m, nil, nil], axis=0).astype(BF16)

    def take_row(s):
        arrived(rows.at[s, FEATS], row_near.at[s])
        prep_row(s)

    def take_col(p):
        arrived(cols.at[p, FEATS], col_near.at[p])
        prep_col(p)

    def take_row_dir(s):
        arrived(rows.at[s, DIRS], row_recv.at[s])
        dir_row[s] = jnp.concatenate(two(rows[s, 0:16, :]), axis=0)

    def take_col_dir(p):
        arrived(cols.at[p, DIRS], col_recv.at[p])
        dir_col[p] = jnp.concatenate(two(cols[p, 0:16, :]), axis=0)

    prep_row(0)
    prep_col(OWN)
    own_dir = jnp.concatenate(two(dir_ref[...]), axis=0)
    dir_row[0] = own_dir
    dir_col[OWN] = own_dir

    def places(t):
        near = jnp.where((t < 6) | (t >= 14), 1, 0)
        pair = jnp.where(t < 6, t, jnp.maximum(t - 8, 0))
        quad = jnp.where(t < 10, t - 6, t - 10)
        base = jnp.where(t < 10, 6, 4)
        first = jnp.where((pair >= 2) & (pair <= 5), 8, 0)
        slots, spots = [], []
        for n in range(4):
            slots.append(jnp.where(near == 1, n if n else first, base + n // 2))
            spots.append([jnp.where(near == 1, 2 * pair + j, 4 * quad + n % 2 * 2 + j) for j in range(2)])
        return near, pair, slots, spots

    def dot(a, b):
        return jnp.dot(a, b, preferred_element_type=F32)

    def dot_t(a, b):
        return lax.dot_general(a, b, LAST, preferred_element_type=F32)

    def distance(s, y):
        return dot(left[s], right[y])

    def spread(d, hi, lo, product):
        both, rest = product(d, hi), product(d[0:16], lo)
        return jnp.concatenate([both[0:16] + rest, both[16:32]], axis=0)

    def work(t, apply, entries, distances):
        near, pair, slots, spots = places(t - 2)
        _, _, slots_n, spots_n = places(t)
        one_way = jnp.where((near == 1) & ((pair == 3) | (pair == 7)), 0.0, 1.0).astype(F32)
        for n in range(4):
            mine = None
            for j in range(2):
                k = n * 2 + j
                if apply:
                    hi, lo = high[k], low[k]
                    term = spread(dir_col[spots[n][j]], hi, lo, dot_t)
                    mine = term if mine is None else mine + term
                    term = spread(dir_row[slots[n]], hi, lo, dot)
                    if n == 0 and j == 1:
                        term = term * one_way
                    acc_col[spots[n][j]] += term
                if entries:
                    hi, lo = two(matern(square[k]))
                    high[k] = hi
                    low[k] = lo
                if distances:
                    square[k] = distance(slots_n[n], spots_n[n][j])
            if apply:
                acc_row[slots[n]] += mine

    def give_row(s):
        return pltpu.make_async_remote_copy(
            src_ref=out_row.at[s], dst_ref=in_row.at[s], send_sem=rs_row_send, recv_sem=rs_row_recv,
            device_id=device(down, across + STEPS[s]), device_id_type=MESH)

    def give_col(p):
        return pltpu.make_async_remote_copy(
            src_ref=out_col.at[p], dst_ref=in_col.at[p], send_sem=rs_col_send, recv_sem=rs_col_recv,
            device_id=device(down + offset_of(p), across), device_id_type=MESH)

    def push_row(s):
        out_row[s] = acc_row[s, 0:16, :] + acc_row[s, 16:32, :]
        give_row(s).start()

    def push_col(p):
        out_col[p] = acc_col[p, 0:16, :] + acc_col[p, 16:32, :]
        give_col(p).start()

    for s in (1, 2, 3):
        take_row(s)
    take_col(0)
    take_col(1)
    work(0, False, False, True)
    take_col(2)
    take_col(3)
    work(1, False, True, True)

    def early(t, _):
        @pl.when(t == 2)
        def _():
            take_row(8)
            for s in (1, 2, 3):
                take_row_dir(s)

        @pl.when(t == 3)
        def _():
            ship((copy_row, DIRS, (6, 7, 4, 5)), (copy_col, DIRS, (8, 9, 10, 11)), (copy_col, FEATS, (12, 13, 14)), (copy_col, DIRS, (12, 13, 14)),)

        @pl.when(t == 4)
        def _():
            take_row_dir(8)

        @pl.when(t == 6)
        def _():
            for s in (4, 5, 6, 7):
                take_row(s)

        take_col_dir(2 * t - 4)
        take_col_dir(2 * t - 3)
        arrived(cols.at[2 * t, FEATS], col_near.at[2 * t])

        @pl.when(t <= 6)
        def _():
            arrived(cols.at[2 * t + 1, FEATS], col_near.at[2 * t + 1])

        for j in range(2):
            prep_col(2 * t + j)
        work(t, True, True, True)
        return 0

    def late(t, _):
        @pl.when(t == 12)
        def _():
            push_row(7)
            push_row(6)

        @pl.when(t >= 13)
        def _():
            for k in range(4):
                push_col(4 * t - 52 + k)

        work(t, True, True, True)
        return 0

    lax.fori_loop(2, 8, early, 0)
    for s in (4, 5, 6, 7):
        take_row_dir(s)
    for p in (12, 13, 14):
        take_col_dir(p)
    push_row(8)
    lax.fori_loop(8, 16, late, 0)
    push_row(5)
    push_row(4)
    work(16, True, True, False)
    push_col(12)
    push_col(13)
    work(17, True, False, False)
    for s in (3, 2, 1):
        push_row(s)
    push_col(14)
    extra = spread(dir_col[7], *two(matern(distance(0, 7))), dot_t)
    extra = extra + spread(dir_row[8], *two(matern(distance(8, OWN))), dot)
    extra = extra + acc_row[0] + acc_col[OWN]
    own = extra[0:16] + extra[16:32]

    arrived(in_col.at[pl.ds(0, SIDE - 1)], rs_col_recv)
    for p in range(SIDE - 1):
        own = own + in_col[p]
    arrived(in_row.at[pl.ds(1, SLOTS - 1)], rs_row_recv)
    for s in range(1, SLOTS):
        own = own + in_row[s]
    direction = dir_ref[...]
    residual = res_ref[...]
    image = CURVE * own + noise_ref[0] * direction

    def total(value):
        return jnp.sum(value, axis=1, keepdims=True)

    lane = lax.broadcasted_iota(jnp.int32, (16, 128), 1) - lax.broadcasted_iota(jnp.int32, (16, 128), 0)
    stats = jnp.zeros((16, 128), F32)
    for k, value in enumerate((residual * residual, direction * image, residual * image, image * image)):
        stats = jnp.where(lane == 16 * k, total(value), stats)
    stats = jnp.sum(stats, axis=0, keepdims=True)
    stat_col[0:1, :] = stats

    def tell_col(y):
        return pltpu.make_async_remote_copy(
            src_ref=stat_col.at[pl.ds(0, 1)], dst_ref=stat_col.at[pl.ds(y, 1)], send_sem=sc_send, recv_sem=sc_recv,
            device_id=device(down + y, across), device_id_type=MESH)

    def tell_row(x):
        return pltpu.make_async_remote_copy(
            src_ref=stat_row.at[pl.ds(0, 1)], dst_ref=stat_row.at[pl.ds(x, 1)], send_sem=sr_send, recv_sem=sr_recv,
            device_id=device(down, across + x), device_id_type=MESH)

    for y in range(1, SIDE):
        tell_col(y).start()
    arrived(stat_col.at[pl.ds(1, SIDE - 1)], sc_recv)
    stats = jnp.sum(stat_col[...], axis=0, keepdims=True)
    stat_row[0:1, :] = stats
    for x in range(1, SIDE):
        tell_row(x).start()
    arrived(stat_row.at[pl.ds(1, SIDE - 1)], sr_recv)
    stats = jnp.sum(stat_row[...], axis=0, keepdims=True)

    def pick(k):
        return total(jnp.where(lane == 16 * k, stats, 0.0))

    rr, pap, cross, squared = pick(0), pick(1), pick(2), pick(3)
    alpha = rr / pap
    rr_next = jnp.maximum(rr - alpha * (2.0 * cross - alpha * squared), 0.0)
    out_ref[0:16, :] = image
    out_ref[16:32, :] = jnp.broadcast_to(alpha, (16, 256))
    out_ref[32:48, :] = jnp.broadcast_to(rr_next / rr, (16, 256))

    arrived(rows.at[pl.ds(1, SLOTS - 1)], row_send)
    arrived(cols.at[pl.ds(0, SIDE - 1)], col_send)
    arrived(out_row.at[pl.ds(1, SLOTS - 1)], rs_row_send)
    arrived(out_col.at[pl.ds(0, SIDE - 1)], rs_col_send)
    arrived(stat_col.at[pl.ds(1, SIDE - 1)], sc_send)
    arrived(stat_row.at[pl.ds(1, SIDE - 1)], sr_send)


def on_device(points, lengthscales, noise, solution, residual, direction):
    vmem = pl.BlockSpec(memory_space=pltpu.VMEM)
    out = jax.ShapeDtypeStruct((16, 256), F32)
    dma = pltpu.SemaphoreType.DMA
    packed = pl.pallas_call(
        kernel,
        out_shape=jax.ShapeDtypeStruct((48, 256), F32),
        in_specs=[pl.BlockSpec(memory_space=pltpu.HBM)] * 6,
        out_specs=vmem,
        scratch_shapes=[
            pltpu.SMEM((11,), F32), pltpu.SMEM((1,), F32), pltpu.VMEM((11, 256), F32),
            pltpu.VMEM((16, 256), F32), pltpu.VMEM((16, 256), F32), pltpu.VMEM((16, 256), F32),
            pltpu.VMEM((SLOTS, 32, 256), F32), pltpu.VMEM((SIDE, 32, 256), F32),
            pltpu.VMEM((SLOTS, 256, 128), BF16), pltpu.VMEM((SIDE, 128, 256), BF16),
            pltpu.VMEM((SLOTS, 32, 256), BF16), pltpu.VMEM((SIDE, 32, 256), BF16),
            pltpu.VMEM((SLOTS, 32, 256), F32), pltpu.VMEM((SIDE, 32, 256), F32),
            pltpu.VMEM((8, 256, 256), F32), pltpu.VMEM((8, 256, 256), BF16), pltpu.VMEM((8, 256, 256), BF16),
            pltpu.VMEM((SLOTS, 16, 256), F32), pltpu.VMEM((SIDE, 16, 256), F32),
            pltpu.VMEM((SLOTS, 16, 256), F32), pltpu.VMEM((SIDE, 16, 256), F32),
            pltpu.VMEM((SIDE, 128), F32), pltpu.VMEM((SIDE, 128), F32), dma((6,)),
            dma, dma((SLOTS,)), dma((SLOTS,)), dma, dma((SIDE,)), dma((SIDE,)),
            dma, dma, dma, dma, dma, dma, dma, dma,
        ],
        compiler_params=pltpu.CompilerParams(
            collective_id=0, has_side_effects=True, vmem_limit_bytes=60 * 2**20),
    )(lengthscales, noise, points, solution, residual, direction)
    image, alpha, beta = packed[0:16], packed[16:32], packed[32:48]
    residual_next = residual - alpha * image
    return solution + alpha * direction, residual_next, residual_next + beta * direction


def solution(mesh):
    placed = (P(None, "blk"), P(), P(), P(None, "blk"), P(None, "blk"), P(None, "blk"))
    return jax.shard_map(
        on_device,
        mesh=mesh,
        in_specs=placed,
        out_specs=(P(None, "blk"), P(None, "blk"), P(None, "blk")),
        check_vma=False,
    )
```

time: 56.2 us -> 54.3 us (0.966)
  Pallas kernels: 53.3 us -> 51.3 us
    pallas_call x1, Pallas kernels: 53.3 us -> 51.3 us  [on_device(): pl.pallas_call(kernel, out_shape=jax.ShapeDtypeStruct((48, 256), F32), in...]
where the time goes in v4:
time: 54.3 us; the launch traced here: 54 us
  Pallas kernels  51.3 us (94%)
  other arithmetic  1.38 us (3%)
  between operations  1.33 us (2%)
    pallas_call x1, Pallas kernels, on_device(): pl.pallas_call(kernel, out_shape=jax.ShapeDtypeStruct((48, 256), F32), in...  51.3 us
    add x1, other arithmetic, on_device(): residual_next + beta * direction  1.38 us

profile of v4, /device:TPU:1, one launch (start us, length us, event | category | flops | bytes accessed | tf_op | source)
XLA Modules:
  0.0 54.0 jit_solution(7628151234704497429)
XLA Ops:
  1.3 0.0 copy-start
  1.3 0.0 copy-start.1
  1.3 0.0 copy-start.2
  1.3 51.3 %shard_map.85 = f32[48,256]{1,0:T(8,128)} custom-call(f32[11]{0:T(128)} %scales_hbm.1, f32[1]{0:T(128)S(6)} %copy.9.noise_hbm, f32[11,256]{1,0:T(8,128)} %points_hbm.1, f32[16,256]{1,0:T(8,128)} %sol_hbm.1, f32[16,256]{1,0:T(8,128)} %res_hbm.1, f32[16,256]{1,0:T(8,128)} %dir_hbm.1), custom_call_target="tpu_custom_call" | custom-call | tf_op jit(solution)/shard_map/pallas_call | solution.py:373
  52.6 0.0 copy-done
  52.6 0.0 copy-done.1
  52.6 0.0 copy-done.2
  52.7 1.4 %multiply_add_fusion = (f32[16,256]{1,0:T(8,128)}, f32[16,256]{1,0:T(8,128)}, f32[16,256]{1,0:T(8,128)}) fusion(f32[16,256]{1,0:T(8,128)S(1)} %copy-done, f32[48,256]{1,0:T(8,128)} %shard_map.85, f32[16,256]{1,0:T(8,128)S(1)} %copy-done.2, f32[16,256]{1,0:T(8,128)S(1)} %copy-done.1), kind=kLoop, calls=%fused_computation | loop fusion | flops 24576 | bytes 147456 | tf_op jit(solution)/shard_map/add | solution.py:397
Async XLA Ops:
  1.3 51.3 %copy-start = (f32[16,256]{1,0:T(8,128)S(1)}, f32[16,256]{1,0:T(8,128)}, u32[]{:S(2)}) copy-start(f32[16,256]{1,0:T(8,128)} %dir_hbm.1) | copy-start | bytes 49156
  1.3 51.3 %copy-start.1 = (f32[16,256]{1,0:T(8,128)S(1)}, f32[16,256]{1,0:T(8,128)}, u32[]{:S(2)}) copy-start(f32[16,256]{1,0:T(8,128)} %sol_hbm.1) | copy-start | bytes 49156
  1.3 51.3 %copy-start.2 = (f32[16,256]{1,0:T(8,128)S(1)}, f32[16,256]{1,0:T(8,128)}, u32[]{:S(2)}) copy-start(f32[16,256]{1,0:T(8,128)} %res_hbm.1) | copy-start | bytes 49156

commit v5 on v4

--- a/solution.py
+++ b/solution.py
@@ -12,6 +12,9 @@
 SIDE = 16
 PLACES = (4, 1, 7, 5, 12, 15, 13, 8, 11, 14, 9, 10, 6, 2, 3, 0)
 OWN = SIDE - 1
+FAR = sorted(
+    ((z, x, y) for z in range(8) for x in range(4) for y in range(4) if z + x + y),
+    key=lambda d: -(min(d[0], 8 - d[0]) + min(d[1], 4 - d[1]) + min(d[2], 4 - d[2])))
 STEPS = (0, 15, 2, 13, 12, 5, 10, 7, 8)
 SLOTS = 9
 LN2 = math.log(2.0)
@@ -45,7 +48,7 @@
     out_ref,
     scales_ref, noise_ref, points_ref, sol_ref, res_ref, dir_ref,
     rows, cols, left, right, dir_row, dir_col, acc_row, acc_col, square, high, low,
-    out_row, out_col, in_row, in_col, stat_col, stat_row, load_sem,
+    out_row, out_col, in_row, in_col, pair_stat, chip_stat, load_sem,
     row_send, row_near, row_recv, col_send, col_near, col_recv, rs_row_send, rs_row_recv, rs_col_send, rs_col_recv,
     sc_send, sc_recv, sr_send, sr_recv,
 ):
@@ -326,27 +329,26 @@
     for k, value in enumerate((residual * residual, direction * image, residual * image, image * image)):
         stats = jnp.where(lane == 16 * k, total(value), stats)
     stats = jnp.sum(stats, axis=0, keepdims=True)
-    stat_col[0:1, :] = stats
-
-    def tell_col(y):
-        return pltpu.make_async_remote_copy(
-            src_ref=stat_col.at[pl.ds(0, 1)], dst_ref=stat_col.at[pl.ds(y, 1)], send_sem=sc_send, recv_sem=sc_recv,
-            device_id=device(down + y, across), device_id_type=MESH)
-
-    def tell_row(x):
-        return pltpu.make_async_remote_copy(
-            src_ref=stat_row.at[pl.ds(0, 1)], dst_ref=stat_row.at[pl.ds(x, 1)], send_sem=sr_send, recv_sem=sr_recv,
-            device_id=device(down, across + x), device_id_type=MESH)
-
-    for y in range(1, SIDE):
-        tell_col(y).start()
-    arrived(stat_col.at[pl.ds(1, SIDE - 1)], sc_recv)
-    stats = jnp.sum(stat_col[...], axis=0, keepdims=True)
-    stat_row[0:1, :] = stats
-    for x in range(1, SIDE):
-        tell_row(x).start()
-    arrived(stat_row.at[pl.ds(1, SIDE - 1)], sr_recv)
-    stats = jnp.sum(stat_row[...], axis=0, keepdims=True)
+
+    core = lax.rem(me, 2)
+    pair_stat[0:1, :] = stats
+    tell_core = pltpu.make_async_remote_copy(
+        src_ref=pair_stat.at[pl.ds(0, 1)], dst_ref=pair_stat.at[pl.ds(8, 1)], send_sem=sc_send, recv_sem=sc_recv,
+        device_id=(me + 1 - 2 * core,), device_id_type=MESH)
+    tell_core.start()
+    zs = [lax.rem(me // 32 + d, 8) * 32 + core for d in range(8)]
+    xs = [lax.rem(me // 8 + d, 4) * 8 for d in range(4)]
+    ys = [lax.rem(me // 2 + d, 4) * 2 for d in range(4)]
+    tell_core.wait_recv()
+    chip_stat[0:1, :] = stats + pair_stat[8:9, :]
+    for k, (dz, dx, dy) in enumerate(FAR):
+        pltpu.make_async_remote_copy(
+            src_ref=chip_stat.at[pl.ds(0, 1)], dst_ref=chip_stat.at[pl.ds(k + 1, 1)],
+            send_sem=sr_send, recv_sem=sr_recv,
+            device_id=(zs[dz] + xs[dx] + ys[dy],), device_id_type=MESH).start()
+    others = chip_stat.at[pl.ds(1, len(FAR))]
+    arrived(others, sr_recv)
+    stats = jnp.sum(chip_stat[...], axis=0, keepdims=True)
 
     def pick(k):
         return total(jnp.where(lane == 16 * k, stats, 0.0))
@@ -362,8 +364,8 @@
     arrived(cols.at[pl.ds(0, SIDE - 1)], col_send)
     arrived(out_row.at[pl.ds(1, SLOTS - 1)], rs_row_send)
     arrived(out_col.at[pl.ds(0, SIDE - 1)], rs_col_send)
-    arrived(stat_col.at[pl.ds(1, SIDE - 1)], sc_send)
-    arrived(stat_row.at[pl.ds(1, SIDE - 1)], sr_send)
+    tell_core.wait_send()
+    arrived(others, sr_send)
 
 
 def on_device(points, lengthscales, noise, solution, residual, direction):
@@ -385,7 +387,7 @@
             pltpu.VMEM((8, 256, 256), F32), pltpu.VMEM((8, 256, 256), BF16), pltpu.VMEM((8, 256, 256), BF16),
             pltpu.VMEM((SLOTS, 16, 256), F32), pltpu.VMEM((SIDE, 16, 256), F32),
             pltpu.VMEM((SLOTS, 16, 256), F32), pltpu.VMEM((SIDE, 16, 256), F32),
-            pltpu.VMEM((SIDE, 128), F32), pltpu.VMEM((SIDE, 128), F32), dma((6,)),
+            pltpu.VMEM((16, 128), F32), pltpu.VMEM((128, 128), F32), dma((6,)),
             dma, dma((SLOTS,)), dma((SLOTS,)), dma, dma((SIDE,)), dma((SIDE,)),
             dma, dma, dma, dma, dma, dma, dma, dma,
         ],

time: 54.3 us -> 52.6 us (0.969)
  Pallas kernels: 51.3 us -> 49.6 us
    pallas_call x1, Pallas kernels: 51.3 us -> 49.6 us  [on_device(): pl.pallas_call(kernel, out_shape=jax.ShapeDtypeStruct((48, 256), F32), in...]
where the time goes in v5:
time: 52.6 us; the launch traced here: 52.3 us
  Pallas kernels  49.6 us (94%)
  other arithmetic  1.38 us (3%)
  between operations  1.33 us (3%)
    pallas_call x1, Pallas kernels, on_device(): pl.pallas_call(kernel, out_shape=jax.ShapeDtypeStruct((48, 256), F32), in...  49.6 us
    add x1, other arithmetic, on_device(): residual_next + beta * direction  1.38 us

profile of v5, /device:TPU:1, one launch (start us, length us, event | category | flops | bytes accessed | tf_op | source)
XLA Modules:
  0.0 52.3 jit_solution(11190205173293384049)
XLA Ops:
  1.3 0.0 copy-start
  1.3 0.0 copy-start.1
  1.3 0.0 copy-start.2
  1.3 49.6 %shard_map.85 = f32[48,256]{1,0:T(8,128)} custom-call(f32[11]{0:T(128)} %scales_hbm.1, f32[1]{0:T(128)S(6)} %copy.9.noise_hbm, f32[11,256]{1,0:T(8,128)} %points_hbm.1, f32[16,256]{1,0:T(8,128)} %sol_hbm.1, f32[16,256]{1,0:T(8,128)} %res_hbm.1, f32[16,256]{1,0:T(8,128)} %dir_hbm.1), custom_call_target="tpu_custom_call" | custom-call | tf_op jit(solution)/shard_map/pallas_call | solution.py:375
  50.9 0.0 copy-done
  51.0 0.0 copy-done.1
  51.0 0.0 copy-done.2
  51.0 1.4 %multiply_add_fusion = (f32[16,256]{1,0:T(8,128)}, f32[16,256]{1,0:T(8,128)}, f32[16,256]{1,0:T(8,128)}) fusion(f32[16,256]{1,0:T(8,128)S(1)} %copy-done, f32[48,256]{1,0:T(8,128)} %shard_map.85, f32[16,256]{1,0:T(8,128)S(1)} %copy-done.2, f32[16,256]{1,0:T(8,128)S(1)} %copy-done.1), kind=kLoop, calls=%fused_computation | loop fusion | flops 24576 | bytes 147456 | tf_op jit(solution)/shard_map/add | solution.py:399
Async XLA Ops:
  1.3 49.7 %copy-start = (f32[16,256]{1,0:T(8,128)S(1)}, f32[16,256]{1,0:T(8,128)}, u32[]{:S(2)}) copy-start(f32[16,256]{1,0:T(8,128)} %dir_hbm.1) | copy-start | bytes 49156
  1.3 49.7 %copy-start.1 = (f32[16,256]{1,0:T(8,128)S(1)}, f32[16,256]{1,0:T(8,128)}, u32[]{:S(2)}) copy-start(f32[16,256]{1,0:T(8,128)} %sol_hbm.1) | copy-start | bytes 49156
  1.3 49.7 %copy-start.2 = (f32[16,256]{1,0:T(8,128)S(1)}, f32[16,256]{1,0:T(8,128)}, u32[]{:S(2)}) copy-start(f32[16,256]{1,0:T(8,128)} %res_hbm.1) | copy-start | bytes 49156

commit v6 on v5

--- a/solution.py
+++ b/solution.py
@@ -44,9 +44,9 @@
 
 
 def kernel(
-    scales_hbm, noise_hbm, points_hbm, sol_hbm, res_hbm, dir_hbm,
+    scales_hbm, noise_hbm, points_hbm, res_hbm, dir_hbm,
     out_ref,
-    scales_ref, noise_ref, points_ref, sol_ref, res_ref, dir_ref,
+    scales_ref, noise_ref, points_ref, res_ref, dir_ref,
     rows, cols, left, right, dir_row, dir_col, acc_row, acc_col, square, high, low,
     out_row, out_col, in_row, in_col, pair_stat, chip_stat, load_sem,
     row_send, row_near, row_recv, col_send, col_near, col_recv, rs_row_send, rs_row_recv, rs_col_send, rs_col_recv,
@@ -80,7 +80,7 @@
         pltpu.make_async_copy(a, b, load_sem.at[k])
         for k, (a, b) in enumerate((
             (points_hbm, points_ref), (scales_hbm, scales_ref), (dir_hbm, dir_ref),
-            (noise_hbm, noise_ref), (sol_hbm, sol_ref), (res_hbm, res_ref)))
+            (noise_hbm, noise_ref), (res_hbm, res_ref)))
     ]
     for load in loads:
         load.start()
@@ -135,14 +135,12 @@
         norm = jnp.sum(jnp.where(line == 11, value, 0.0), axis=0, keepdims=True)
         value = jnp.where(line == 11, 1.0, jnp.where(line == 12, norm, -2.0 * value))
         h, m, l = three(value)
-        nil = jnp.zeros((SIDE, 256), F32)
-        tall = jnp.concatenate([h, h, m, h, l, m, nil, nil], axis=0)
+        tall = jnp.concatenate([h, h, m, h, l, m], axis=0)
         left[s] = jnp.transpose(tall).astype(BF16)
 
     def prep_col(p):
         h, m, l = three(cols[p, 16:32, :])
-        nil = jnp.zeros((SIDE, 256), F32)
-        right[p] = jnp.concatenate([h, m, h, l, h, m, nil, nil], axis=0).astype(BF16)
+        right[p] = jnp.concatenate([h, m, h, l, h, m], axis=0).astype(BF16)
 
     def take_row(s):
         arrived(rows.at[s, FEATS], row_near.at[s])
@@ -156,9 +154,12 @@
         arrived(rows.at[s, DIRS], row_recv.at[s])
         dir_row[s] = jnp.concatenate(two(rows[s, 0:16, :]), axis=0)
 
+    def split_col_dir(p):
+        dir_col[p] = jnp.concatenate(two(cols[p, 0:16, :]), axis=0)
+
     def take_col_dir(p):
         arrived(cols.at[p, DIRS], col_recv.at[p])
-        dir_col[p] = jnp.concatenate(two(cols[p, 0:16, :]), axis=0)
+        split_col_dir(p)
 
     prep_row(0)
     prep_col(OWN)
@@ -263,8 +264,8 @@
             for s in (4, 5, 6, 7):
                 take_row(s)
 
-        take_col_dir(2 * t - 4)
-        take_col_dir(2 * t - 3)
+        for j in range(2):
+            arrived(cols.at[2 * t - 4 + j, DIRS], col_recv.at[2 * t - 4 + j])
         arrived(cols.at[2 * t, FEATS], col_near.at[2 * t])
 
         @pl.when(t <= 6)
@@ -272,6 +273,7 @@
             arrived(cols.at[2 * t + 1, FEATS], col_near.at[2 * t + 1])
 
         for j in range(2):
+            split_col_dir(2 * t - 4 + j)
             prep_col(2 * t + j)
         work(t, True, True, True)
         return 0
@@ -375,25 +377,25 @@
     packed = pl.pallas_call(
         kernel,
         out_shape=jax.ShapeDtypeStruct((48, 256), F32),
-        in_specs=[pl.BlockSpec(memory_space=pltpu.HBM)] * 6,
+        in_specs=[pl.BlockSpec(memory_space=pltpu.HBM)] * 5,
         out_specs=vmem,
         scratch_shapes=[
             pltpu.SMEM((11,), F32), pltpu.SMEM((1,), F32), pltpu.VMEM((11, 256), F32),
-            pltpu.VMEM((16, 256), F32), pltpu.VMEM((16, 256), F32), pltpu.VMEM((16, 256), F32),
+            pltpu.VMEM((16, 256), F32), pltpu.VMEM((16, 256), F32),
             pltpu.VMEM((SLOTS, 32, 256), F32), pltpu.VMEM((SIDE, 32, 256), F32),
-            pltpu.VMEM((SLOTS, 256, 128), BF16), pltpu.VMEM((SIDE, 128, 256), BF16),
+            pltpu.VMEM((SLOTS, 256, 96), BF16), pltpu.VMEM((SIDE, 96, 256), BF16),
             pltpu.VMEM((SLOTS, 32, 256), BF16), pltpu.VMEM((SIDE, 32, 256), BF16),
             pltpu.VMEM((SLOTS, 32, 256), F32), pltpu.VMEM((SIDE, 32, 256), F32),
             pltpu.VMEM((8, 256, 256), F32), pltpu.VMEM((8, 256, 256), BF16), pltpu.VMEM((8, 256, 256), BF16),
             pltpu.VMEM((SLOTS, 16, 256), F32), pltpu.VMEM((SIDE, 16, 256), F32),
             pltpu.VMEM((SLOTS, 16, 256), F32), pltpu.VMEM((SIDE, 16, 256), F32),
-            pltpu.VMEM((16, 128), F32), pltpu.VMEM((128, 128), F32), dma((6,)),
+            pltpu.VMEM((16, 128), F32), pltpu.VMEM((128, 128), F32), dma((5,)),
             dma, dma((SLOTS,)), dma((SLOTS,)), dma, dma((SIDE,)), dma((SIDE,)),
             dma, dma, dma, dma, dma, dma, dma, dma,
         ],
         compiler_params=pltpu.CompilerParams(
             collective_id=0, has_side_effects=True, vmem_limit_bytes=60 * 2**20),
-    )(lengthscales, noise, points, solution, residual, direction)
+    )(lengthscales, noise, points, residual, direction)
     image, alpha, beta = packed[0:16], packed[16:32], packed[32:48]
     residual_next = residual - alpha * image
     return solution + alpha * direction, residual_next, residual_next + beta * direction

time: 52.6 us -> 52.2 us (level)
  no operation moved by 1% of the time
where the time goes in v6:
time: 52.2 us; the launch traced here: 51.9 us
  Pallas kernels  49.2 us (94%)
  other arithmetic  1.38 us (3%)
  between operations  1.33 us (3%)
    pallas_call x1, Pallas kernels, on_device(): pl.pallas_call(kernel, out_shape=jax.ShapeDtypeStruct((48, 256), F32), in...  49.2 us
    add x1, other arithmetic, on_device(): residual_next + beta * direction  1.38 us

profile of v6, /device:TPU:1, one launch (start us, length us, event | category | flops | bytes accessed | tf_op | source)
XLA Modules:
  0.0 51.9 jit_solution(1252588297074062520)
XLA Ops:
  1.3 0.0 copy-start
  1.3 0.0 copy-start.1
  1.3 0.0 copy-start.2
  1.3 49.2 %shard_map.85 = f32[48,256]{1,0:T(8,128)} custom-call(f32[11]{0:T(128)} %scales_hbm.1, f32[1]{0:T(128)S(6)} %copy.9.noise_hbm, f32[11,256]{1,0:T(8,128)} %points_hbm.1, f32[16,256]{1,0:T(8,128)} %res_hbm.1, f32[16,256]{1,0:T(8,128)} %dir_hbm.1), custom_call_target="tpu_custom_call" | custom-call | tf_op jit(solution)/shard_map/pallas_call | solution.py:377
  50.5 0.0 copy-done
  50.5 0.0 copy-done.1
  50.6 0.0 copy-done.2
  50.6 1.4 %multiply_add_fusion = (f32[16,256]{1,0:T(8,128)}, f32[16,256]{1,0:T(8,128)}, f32[16,256]{1,0:T(8,128)}) fusion(f32[16,256]{1,0:T(8,128)S(1)} %copy-done, f32[48,256]{1,0:T(8,128)} %shard_map.85, f32[16,256]{1,0:T(8,128)S(1)} %copy-done.1, f32[16,256]{1,0:T(8,128)S(1)} %copy-done.2), kind=kLoop, calls=%fused_computation | loop fusion | flops 24576 | bytes 147456 | tf_op jit(solution)/shard_map/add | solution.py:401
Async XLA Ops:
  1.3 49.3 %copy-start = (f32[16,256]{1,0:T(8,128)S(1)}, f32[16,256]{1,0:T(8,128)}, u32[]{:S(2)}) copy-start(f32[16,256]{1,0:T(8,128)} %dir_hbm.1) | copy-start | bytes 49156
  1.3 49.3 %copy-start.1 = (f32[16,256]{1,0:T(8,128)S(1)}, f32[16,256]{1,0:T(8,128)}, u32[]{:S(2)}) copy-start(f32[16,256]{1,0:T(8,128)} %res_hbm.1) | copy-start | bytes 49156
  1.3 49.3 %copy-start.2 = (f32[16,256]{1,0:T(8,128)S(1)}, f32[16,256]{1,0:T(8,128)}, u32[]{:S(2)}) copy-start(f32[16,256]{1,0:T(8,128)} %param.9) | copy-start | bytes 49156

commit v7 on v6

--- a/solution.py
+++ b/solution.py
@@ -10,7 +10,7 @@
 MESH = pl.DeviceIdType.MESH
 F32, BF16 = jnp.float32, jnp.bfloat16
 SIDE = 16
-PLACES = (4, 1, 7, 5, 12, 15, 13, 8, 11, 14, 9, 10, 6, 2, 3, 0)
+PLACES = (4, 1, 7, 6, 12, 15, 13, 8, 11, 14, 9, 10, 5, 2, 3, 0)
 OWN = SIDE - 1
 FAR = sorted(
     ((z, x, y) for z in range(8) for x in range(4) for y in range(4) if z + x + y),
@@ -129,6 +129,7 @@
                 make(k, part).start()
 
     ship((copy_row, FEATS, (1, 2, 3)), (copy_col, FEATS, (0, 1, 2, 3)), (copy_row, DIRS, (1, 2, 3)), (copy_row, FEATS, (8,)), (copy_col, FEATS, (4, 5, 6, 7)), (copy_col, DIRS, (0, 1, 2, 3)), (copy_row, FEATS, (6, 7, 4, 5)), (copy_col, FEATS, (8, 9, 10, 11)), (copy_row, DIRS, (8,)), (copy_col, DIRS, (4, 5, 6, 7)),)
+    ship((copy_row, DIRS, (6, 7, 4, 5)), (copy_col, DIRS, (8, 9, 10, 11)), (copy_col, FEATS, (12, 13, 14)), (copy_col, DIRS, (12, 13, 14)),)
 
     def prep_row(s):
         value = rows[s, 16:32, :]
@@ -250,10 +251,6 @@
             take_row(8)
             for s in (1, 2, 3):
                 take_row_dir(s)
-
-        @pl.when(t == 3)
-        def _():
-            ship((copy_row, DIRS, (6, 7, 4, 5)), (copy_col, DIRS, (8, 9, 10, 11)), (copy_col, FEATS, (12, 13, 14)), (copy_col, DIRS, (12, 13, 14)),)
 
         @pl.when(t == 4)
         def _():

time: 52.2 us -> 52 us (level)
  no operation moved by 1% of the time
where the time goes in v7:
time: 52 us; the launch traced here: 51.7 us
  Pallas kernels  49 us (94%)
  other arithmetic  1.38 us (3%)
  between operations  1.33 us (3%)
    pallas_call x1, Pallas kernels, on_device(): pl.pallas_call(kernel, out_shape=jax.ShapeDtypeStruct((48, 256), F32), in...  49 us
    add x1, other arithmetic, on_device(): residual_next + beta * direction  1.38 us

profile of v7, /device:TPU:1, one launch (start us, length us, event | category | flops | bytes accessed | tf_op | source)
XLA Modules:
  0.0 51.7 jit_solution(5969513837849346108)
XLA Ops:
  1.3 0.0 copy-start
  1.3 0.0 copy-start.1
  1.3 0.0 copy-start.2
  1.3 49.0 %shard_map.85 = f32[48,256]{1,0:T(8,128)} custom-call(f32[11]{0:T(128)} %scales_hbm.1, f32[1]{0:T(128)S(6)} %copy.9.noise_hbm, f32[11,256]{1,0:T(8,128)} %points_hbm.1, f32[16,256]{1,0:T(8,128)} %res_hbm.1, f32[16,256]{1,0:T(8,128)} %dir_hbm.1), custom_call_target="tpu_custom_call" | custom-call | tf_op jit(solution)/shard_map/pallas_call | solution.py:374
  50.3 0.0 copy-done
  50.3 0.0 copy-done.1
  50.4 0.0 copy-done.2
  50.4 1.4 %multiply_add_fusion = (f32[16,256]{1,0:T(8,128)}, f32[16,256]{1,0:T(8,128)}, f32[16,256]{1,0:T(8,128)}) fusion(f32[16,256]{1,0:T(8,128)S(1)} %copy-done, f32[48,256]{1,0:T(8,128)} %shard_map.85, f32[16,256]{1,0:T(8,128)S(1)} %copy-done.1, f32[16,256]{1,0:T(8,128)S(1)} %copy-done.2), kind=kLoop, calls=%fused_computation | loop fusion | flops 24576 | bytes 147456 | tf_op jit(solution)/shard_map/add | solution.py:398
Async XLA Ops:
  1.3 49.1 %copy-start = (f32[16,256]{1,0:T(8,128)S(1)}, f32[16,256]{1,0:T(8,128)}, u32[]{:S(2)}) copy-start(f32[16,256]{1,0:T(8,128)} %dir_hbm.1) | copy-start | bytes 49156
  1.3 49.1 %copy-start.1 = (f32[16,256]{1,0:T(8,128)S(1)}, f32[16,256]{1,0:T(8,128)}, u32[]{:S(2)}) copy-start(f32[16,256]{1,0:T(8,128)} %res_hbm.1) | copy-start | bytes 49156
  1.3 49.1 %copy-start.2 = (f32[16,256]{1,0:T(8,128)S(1)}, f32[16,256]{1,0:T(8,128)}, u32[]{:S(2)}) copy-start(f32[16,256]{1,0:T(8,128)} %param.9) | copy-start | bytes 49156
